TPU v7x, 32 devices: a whole 2x2x4 slice. The times are simulated.
32 devices in a mesh: seq: 8 (over z, x), fsdp: 4 (over y, core).
Axes of the slice: x: 2, y: 2, z: 4, core: 2. Of those that a mesh axis runs over, the one named last changes fastest.
Arguments:
- tokens: bfloat16 [4, 8192, 1024], P('fsdp', 'seq'), may hold values from -6 to 6
- cotangent: bfloat16 [4, 8192, 1024], P('fsdp', 'seq'), may hold values from -6 to 6
- lengths: int32 [4], P('fsdp'), may hold values from 2048 to 8192, as said below
- triple_weight: float32 [1024, 3072], P('seq', 'fsdp'), may hold values from -0.1875 to 0.1875
- output_weight: float32 [1024, 1024], P('seq', 'fsdp'), may hold values from -6 to 6
- expand_weight: float32 [1024, 5248], P('seq', 'fsdp'), may hold values from -0.1875 to 0.1875
- shrink_weight: float32 [2624, 1024], P('fsdp', 'seq'), may hold values from -0.125 to 0.125
- norm_gains: float32 [2, 1024], replicated, may hold values from 0.5 to 1.5
- side_bases: float32 [4, 1024, 1024], P(None, 'seq'), may hold values from -1 to 1, as said below
- output_right: float32 [1024, 1024], P('fsdp'), may hold values from -1 to 1, as said below
- triple_first: float32 [1024, 3072], P('seq', 'fsdp'), may hold values from -28 to 28
- triple_second: float32 [1024, 3072], P('seq', 'fsdp'), may hold values from 409.6 to 1638.4
- output_first: float32 [1024, 1024], P('seq', 'fsdp'), may hold values from -2.5 to 2.5
- output_second: float32 [1024, 1024], P('seq', 'fsdp'), may hold values from 0.52 to 2
- expand_first: float32 [1024, 5248], P('seq', 'fsdp'), may hold values from -16 to 16
- expand_second: float32 [1024, 5248], P('seq', 'fsdp'), may hold values from 147.456 to 589.824
- shrink_first: float32 [2624, 1024], P('fsdp', 'seq'), may hold values from -28 to 28
- shrink_second: float32 [2624, 1024], P('fsdp', 'seq'), may hold values from 409.6 to 1638.4
- gains_first: float32 [2, 1024], replicated, may hold values from -32 to 32
- gains_second: float32 [2, 1024], replicated, may hold values from 589.824 to 2359.296
Outputs:
- mixed: bfloat16 [4, 8192, 1024], P('fsdp', 'seq')
- token_gradient: bfloat16 [4, 8192, 1024], P('fsdp', 'seq')
- triple_gradient: float32 [1024, 3072], P('seq', 'fsdp')
- output_gradient: float32 [1024, 1024], P('seq', 'fsdp')
- expand_gradient: float32 [1024, 5248], P('seq', 'fsdp')
- shrink_gradient: float32 [2624, 1024], P('fsdp', 'seq')
- gains_gradient: float32 [2, 1024], replicated
- triple_average: float32 [1024, 3072], P('seq', 'fsdp')
- triple_variance: float32 [1024, 3072], P('seq', 'fsdp')
- triple_updated: float32 [1024, 3072], P('seq', 'fsdp')
- triple_copy: bfloat16 [1024, 3072], P('seq', 'fsdp')
- output_average: float32 [1024, 1024], P('seq', 'fsdp')
- output_variance: float32 [1024, 1024], P('seq', 'fsdp')
- output_updated: float32 [1024, 1024], P('seq', 'fsdp')
- output_copy: bfloat16 [1024, 1024], P('seq', 'fsdp')
- expand_average: float32 [1024, 5248], P('seq', 'fsdp')
- expand_variance: float32 [1024, 5248], P('seq', 'fsdp')
- expand_updated: float32 [1024, 5248], P('seq', 'fsdp')
- expand_copy: bfloat16 [1024, 5248], P('seq', 'fsdp')
- shrink_average: float32 [2624, 1024], P('fsdp', 'seq')
- shrink_variance: float32 [2624, 1024], P('fsdp', 'seq')
- shrink_updated: float32 [2624, 1024], P('fsdp', 'seq')
- shrink_copy: bfloat16 [2624, 1024], P('fsdp', 'seq')
- gains_average: float32 [2, 1024], replicated
- gains_variance: float32 [2, 1024], replicated
- gains_updated: float32 [2, 1024], replicated
Inputs may be any that keep to these rules, and one draw needn't show every extreme that they name: Row r holds one sequence in its first lengths[r] slots, the rest is padding; some row is full. `side_bases`: each of the four matrices is orthogonal. `output_right`: orthogonal.
All inputs are finite; a program needn't handle non-finite values.
Results may differ from a plain program's by a relative error of at most 0.028.
Values may be sent and summed in bfloat16 or wider, within the bound.
No kernel may reach another device: no remote copies, remote signals or barrier semaphores. Data moves between devices by JAX's collectives and lax.ppermute only.
A program may use at most 448 MiB of HBM per device.

v0:
```python
import functools
import math

import jax
import jax.numpy as jnp
from jax import lax
from jax.experimental import pallas as pl
from jax.experimental.pallas import tpu as pltpu
from jax.sharding import Mesh
from jax.sharding import PartitionSpec as P

HEADS = 16
HEAD_DIM = 64
FF = 2624
STEP = 10


ROPE_BASE = 160000.0
NORM_EPS = 1e-05
NEG_LARGE = -1e30
BETA_ONE = 0.95
BETA_TWO = 0.95
ADAM_EPS = 1e-08
DECAY_RATE = 0.01
WEIGHT_RATES = (0.03, 1.0, 0.03, 0.03)
GAINS_RATE = 0.8


def layer_norm(values, gain):
    centre = values - jnp.mean(values, axis=-1, keepdims=True)
    spread = jnp.mean(centre * centre, axis=-1, keepdims=True)
    return centre * lax.rsqrt(spread + NORM_EPS) * gain


def rotary_tables(position):
    halves = HEAD_DIM // 2
    frequency = ROPE_BASE ** (-2.0 * jnp.arange(halves, dtype=jnp.float32) / HEAD_DIM)
    angle = frequency[:, None] * position.astype(jnp.float32)[None, :]
    return jnp.cos(angle), jnp.sin(angle)


def outer_sum(left, right):
    return lax.dot_general(
        left, right, (((0,), (0,)), ((), ())), preferred_element_type=jnp.float32
    )


def back_product(left, right):
    return lax.dot_general(
        left, right, (((1,), (1,)), ((), ())), preferred_element_type=jnp.float32
    )


def plain_product(left, right):
    return jnp.dot(left, right, preferred_element_type=jnp.float32)


NT = (((1,), (1,)), ((), ()))
SAFE_BOUND = 60.0
MASK = -1e30
VMEM_LIMIT = 60 * 1024 * 1024


def extra_rows(rows, length, size=HEAD_DIM):
    place = lax.broadcasted_iota(jnp.int32, (size, length), 0)
    block = jnp.zeros((size, length), jnp.float32)
    for index, row in enumerate(rows):
        block = jnp.where(place == index, row, block)
    return block.astype(jnp.bfloat16)


def three_parts(row):
    high = row.astype(jnp.bfloat16).astype(jnp.float32)
    middle = (row - high).astype(jnp.bfloat16).astype(jnp.float32)
    return [high, middle, row - high - middle]


def mask_row(start, length, limit):
    place = start + lax.broadcasted_iota(jnp.int32, (1, length), 1)
    return jnp.where(place < limit, 0.0, MASK)


def project_kernel(pieces_ref, first_ref, cosine_ref, sine_ref, out_ref, rows_ref):
    shards, _, heads = pieces_ref.shape[:3]
    lanes = pieces_ref.shape[-1]
    weight = jnp.concatenate(
        [pieces_ref[shard].reshape(3 * heads * HEAD_DIM, lanes) for shard in range(shards)], axis=1
    )
    product = lax.dot_general(weight, first_ref[...], NT, preferred_element_type=jnp.float32)
    cosine, sine = cosine_ref[...], sine_ref[...]
    half = HEAD_DIM // 2
    for head in range(heads):
        for part in range(3):
            base = (part * heads + head) * HEAD_DIM
            rows_ref[head, part] = weight[base : base + HEAD_DIM]
        for part, scale in ((0, HEAD_DIM**-0.5), (1, 1.0)):
            base = (part * heads + head) * HEAD_DIM
            upper, lower = product[base : base + half], product[base + half : base + HEAD_DIM]
            turned_upper = (upper * cosine - lower * sine).astype(jnp.bfloat16)
            turned_lower = (lower * cosine + upper * sine).astype(jnp.bfloat16)
            place = part * HEAD_DIM
            out_ref[head, place : place + half, :] = turned_upper * jnp.bfloat16(scale)
            out_ref[head, place + half : place + HEAD_DIM, :] = turned_lower * jnp.bfloat16(
                scale
            )
        base = (2 * heads + head) * HEAD_DIM
        out_ref[head, 2 * HEAD_DIM :, :] = product[base : base + HEAD_DIM].astype(jnp.bfloat16)


def project_heads(pieces, first, cosine, sine):
    shards, lanes = pieces.shape[0], pieces.shape[-1]
    count, width = first.shape
    pieces = pieces.reshape(shards, 3, shards, HEAD_DIM, lanes)
    group = min(4, shards)
    half = HEAD_DIM // 2
    return pl.pallas_call(
        project_kernel,
        grid=(shards // group,),
        in_specs=[
            pl.BlockSpec(
                (shards, 3, group, HEAD_DIM, lanes), lambda g: (0, 0, g, 0, 0)
            ),
            pl.BlockSpec((count, width), lambda g: (0, 0)),
            pl.BlockSpec((half, count), lambda g: (0, 0)),
            pl.BlockSpec((half, count), lambda g: (0, 0)),
        ],
        out_specs=[
            pl.BlockSpec((group, 3 * HEAD_DIM, count), lambda g: (g, 0, 0)),
            pl.BlockSpec((group, 3, HEAD_DIM, width), lambda g: (g, 0, 0, 0)),
        ],
        out_shape=[
            jax.ShapeDtypeStruct((shards, 3 * HEAD_DIM, count), jnp.bfloat16),
            jax.ShapeDtypeStruct((shards, 3, HEAD_DIM, width), jnp.bfloat16),
        ],
        compiler_params=pltpu.CompilerParams(vmem_limit_bytes=VMEM_LIMIT),
        cost_estimate=pl.CostEstimate(
            flops=6 * width * shards * HEAD_DIM * count,
            bytes_accessed=20 * width * shards * HEAD_DIM,
            transcendentals=0,
        ),
    )(pieces, first, cosine, sine)


def forward_kernel(
    length_ref,
    own_ref,
    other_ref,
    out_ref,
    log_ref,
    query_ref,
    key_ref,
    value_ref,
    peak_ref,
    bound_ref,
):
    row, index = pl.program_id(0), pl.program_id(1)
    shards, _, local = own_ref.shape
    limit = length_ref[row]
    ratio = max(1, 2048 // local)
    blocks = (limit + local - 1) // local

    def prepare(joint_ref, first):
        query_most = jnp.zeros((1, 1), jnp.float32)
        key_most = jnp.zeros((1, 1), jnp.float32)
        for shard in range(shards):
            place = slice(shard * local, (shard + 1) * local)
            key = joint_ref[shard, HEAD_DIM : 2 * HEAD_DIM, :]
            wide_key = key.astype(jnp.float32)
            key_size = jnp.sum(wide_key * wide_key, axis=0, keepdims=True)
            key_most = jnp.maximum(key_most, jnp.max(key_size, axis=1, keepdims=True))
            extra = extra_rows([mask_row(shard * local, local, limit), 1.0], local)
            key_ref[place, :] = jnp.concatenate([key, extra], axis=0).T
            value_ref[:HEAD_DIM, place] = joint_ref[shard, 2 * HEAD_DIM :, :]
            value_ref[HEAD_DIM:, place] = extra_rows([1.0], local, 16)
        for block in range(shards // 2):
            query = joint_ref[2 * block + first, :HEAD_DIM, :]
            wide_query = query.astype(jnp.float32)
            query_size = jnp.sum(wide_query * wide_query, axis=0, keepdims=True)
            query_most = jnp.maximum(query_most, jnp.max(query_size, axis=1, keepdims=True))
            query_ref[block] = query
        bound_ref[0] = (jnp.sqrt(query_most) * jnp.sqrt(key_most))[0, 0]

    for which, joint_ref in enumerate((own_ref, other_ref)):
        pl.when((index == 0) & (row == which))(
            functools.partial(prepare, joint_ref, which)
        )

    mine = 2 * index + row < blocks

    @pl.when(jnp.logical_not(mine))
    def padding():
        out_ref[...] = jnp.zeros_like(out_ref)
        log_ref[...] = jnp.zeros_like(log_ref)

    @pl.when(mine)
    def compute():
        query = query_ref[index]
        peak_ref[...] = jnp.zeros_like(peak_ref)

        @pl.when(bound_ref[0] > SAFE_BOUND)
        def find_peak():
            plain = jnp.concatenate([query, extra_rows([1.0], local)], axis=0)

            def step(block, peak):
                place = pl.ds(pl.multiple_of(block * local, local), local)
                scores = jnp.dot(key_ref[place, :], plain, preferred_element_type=jnp.float32)
                return jnp.maximum(peak, jnp.max(scores, axis=0, keepdims=True))

            peak = lax.fori_loop(0, blocks, step, jnp.full((1, local), MASK, jnp.float32))
            peak_ref[...] = peak.astype(jnp.bfloat16).astype(jnp.float32)

        peak = peak_ref[...]
        augmented = jnp.concatenate([query, extra_rows([1.0, -peak], local)], axis=0)

        def attend(start, size, total):
            place = pl.ds(pl.multiple_of(start, local), size)
            scores = jnp.dot(key_ref[place, :], augmented, preferred_element_type=jnp.float32)
            weights = jnp.exp(scores).astype(jnp.bfloat16)
            return total + jnp.dot(
                value_ref[:, place], weights, preferred_element_type=jnp.float32
            )

        large = blocks // ratio
        total = lax.fori_loop(
            0,
            large,
            lambda block, total: attend(block * (ratio * local), ratio * local, total),
            jnp.zeros((HEAD_DIM + 16, local), jnp.float32),
        )
        total = lax.fori_loop(
            large * ratio, blocks, lambda block, total: attend(block * local, local, total), total
        )
        mass = total[HEAD_DIM : HEAD_DIM + 1, :]
        out_ref[0, 0] = (total[:HEAD_DIM, :] / mass).astype(jnp.bfloat16)
        log_ref[0, 0] = peak + jnp.log(mass)


def attend_forward(lengths, own, other):
    shards, _, local = own.shape
    total = shards * local
    half = shards // 2
    joint = pl.BlockSpec((shards, 3 * HEAD_DIM, local), lambda r, i: (0, 0, 0))
    return pl.pallas_call(
        forward_kernel,
        grid=(2, half),
        in_specs=[pl.BlockSpec(memory_space=pltpu.SMEM), joint, joint],
        out_specs=[
            pl.BlockSpec((1, 1, HEAD_DIM, local), lambda r, i: (r, i, 0, 0)),
            pl.BlockSpec((1, 1, 1, local), lambda r, i: (r, i, 0, 0)),
        ],
        out_shape=[
            jax.ShapeDtypeStruct((2, half, HEAD_DIM, local), jnp.bfloat16),
            jax.ShapeDtypeStruct((2, half, 1, local), jnp.float32),
        ],
        scratch_shapes=[
            pltpu.VMEM((half, HEAD_DIM, local), jnp.bfloat16),
            pltpu.VMEM((total, 2 * HEAD_DIM), jnp.bfloat16),
            pltpu.VMEM((HEAD_DIM + 16, total), jnp.bfloat16),
            pltpu.VMEM((1, local), jnp.float32),
            pltpu.SMEM((1,), jnp.float32),
        ],
        compiler_params=pltpu.CompilerParams(vmem_limit_bytes=VMEM_LIMIT),
        cost_estimate=pl.CostEstimate(
            flops=total * total,
            bytes_accessed=HEAD_DIM * total,
            transcendentals=0,
        ),
    )(lengths, own, other)


def backward_kernel(
    length_ref,
    own_ref,
    other_ref,
    own_back_ref,
    other_back_ref,
    out_ref,
    log_ref,
    cosine_ref,
    sine_ref,
    own_grad_ref,
    other_grad_ref,
    query_ref,
    wide_ref,
    query_flat,
    back_flat,
    query_sum,
):
    row, index = pl.program_id(0), pl.program_id(1)
    shards, _, local = own_ref.shape
    limit = length_ref[row]
    ratio = max(1, 2048 // local)
    blocks = (limit + local - 1) // local
    mine = (blocks + 1 - row) // 2
    half = HEAD_DIM // 2

    def turned_back(wide, shard):
        cosine, sine = cosine_ref[shard], sine_ref[shard]
        upper, lower = wide[:half], wide[half:]
        return jnp.concatenate(
            [upper * cosine + lower * sine, lower * cosine - upper * sine], axis=0
        ).astype(jnp.bfloat16)

    def prepare(joint_ref, back_ref, first):
        for block in range(shards // 2):
            place = slice(block * local, (block + 1) * local)
            query = joint_ref[2 * block + first, :HEAD_DIM, :]
            back = back_ref[2 * block + first]
            extra = extra_rows([1.0] + three_parts(-log_ref[first, block]), local)
            query_ref[place, :] = jnp.concatenate([query, extra], axis=0).T
            balance = jnp.sum(
                back.astype(jnp.float32) * out_ref[first, block].astype(jnp.float32),
                axis=0,
                keepdims=True,
            )
            extra = extra_rows(three_parts(-balance), local)
            wide_ref[place, :] = jnp.concatenate([back, extra], axis=0).T
            query_flat[:, place] = query
            back_flat[:, place] = back
        query_sum[...] = jnp.zeros_like(query_sum)

    def work(joint_ref, grad_ref):
        key = joint_ref[index, HEAD_DIM : 2 * HEAD_DIM, :]
        value = joint_ref[index, 2 * HEAD_DIM :, :]
        mask = mask_row(index * local, local, limit)
        wide_key = jnp.concatenate([key, extra_rows([mask, 1.0, 1.0, 1.0], local)], axis=0)
        wide_value = jnp.concatenate([value, extra_rows([1.0, 1.0, 1.0], local)], axis=0)

        def gather(start, size, carry):
            key_sum, value_sum = carry
            place = pl.ds(pl.multiple_of(start, local), size)
            scores = jnp.dot(query_ref[place, :], wide_key, preferred_element_type=jnp.float32)
            chance = jnp.exp(scores)
            change = jnp.dot(wide_ref[place, :], wide_value, preferred_element_type=jnp.float32)
            chance_low = chance.astype(jnp.bfloat16)
            score_back = (chance * change).astype(jnp.bfloat16)
            value_sum = value_sum + jnp.dot(
                back_flat[:, place], chance_low, preferred_element_type=jnp.float32
            )
            key_sum = key_sum + jnp.dot(
                query_flat[:, place], score_back, preferred_element_type=jnp.float32
            )
            query_sum[:, place] += lax.dot_general(
                key, score_back, NT, preferred_element_type=jnp.float32
            )
            return (key_sum, value_sum)

        large = mine // ratio
        zero = jnp.zeros((HEAD_DIM, local), jnp.float32)
        carry = lax.fori_loop(
            0,
            large,
            lambda block, carry: gather(block * (ratio * local), ratio * local, carry),
            (zero, zero),
        )
        key_sum, value_sum = lax.fori_loop(
            large * ratio, mine, lambda block, carry: gather(block * local, local, carry), carry
        )
        grad_ref[index, HEAD_DIM : 2 * HEAD_DIM, :] = turned_back(key_sum, index)
        grad_ref[index, 2 * HEAD_DIM :, :] = value_sum.astype(jnp.bfloat16)

    def padding(grad_ref):
        grad_ref[index, HEAD_DIM:, :] = jnp.zeros((2 * HEAD_DIM, local), jnp.bfloat16)

    def finish(grad_ref, first):
        for block in range(shards // 2):
            place = slice(block * local, (block + 1) * local)
            shard = 2 * block + first
            grad_ref[shard, :HEAD_DIM, :] = turned_back(
                query_sum[:, place] * HEAD_DIM**-0.5, shard
            )
            grad_ref[shard + 1 - 2 * first, :HEAD_DIM, :] = jnp.zeros(
                (HEAD_DIM, local), jnp.bfloat16
            )

    sides = ((own_ref, own_back_ref, own_grad_ref), (other_ref, other_back_ref, other_grad_ref))
    for which, (joint_ref, back_ref, grad_ref) in enumerate(sides):
        here = row == which
        pl.when(here & (index == 0))(functools.partial(prepare, joint_ref, back_ref, which))
        pl.when(here & (index < blocks))(functools.partial(work, joint_ref, grad_ref))
        pl.when(here & (index >= blocks))(functools.partial(padding, grad_ref))
        pl.when(here & (index == shards - 1))(functools.partial(finish, grad_ref, which))


def attend_backward(lengths, own, other, own_back, other_back, out, log_mass, cosine, sine):
    shards, _, local = own.shape
    total = shards * local
    half = shards // 2
    whole = lambda *shape: pl.BlockSpec(shape, lambda r, i: (0,) * len(shape))
    grad = jax.ShapeDtypeStruct((shards, 3 * HEAD_DIM, local), jnp.bfloat16)
    return pl.pallas_call(
        backward_kernel,
        grid=(2, shards),
        in_specs=[pl.BlockSpec(memory_space=pltpu.SMEM)]
        + [whole(shards, 3 * HEAD_DIM, local)] * 2
        + [whole(shards, HEAD_DIM, local)] * 2
        + [whole(2, half, HEAD_DIM, local), whole(2, half, 1, local)]
        + [whole(shards, HEAD_DIM // 2, local)] * 2,
        out_specs=[whole(shards, 3 * HEAD_DIM, local)] * 2,
        out_shape=[grad, grad],
        scratch_shapes=[
            pltpu.VMEM((total // 2, 2 * HEAD_DIM), jnp.bfloat16),
            pltpu.VMEM((total // 2, 2 * HEAD_DIM), jnp.bfloat16),
            pltpu.VMEM((HEAD_DIM, total // 2), jnp.bfloat16),
            pltpu.VMEM((HEAD_DIM, total // 2), jnp.bfloat16),
            pltpu.VMEM((HEAD_DIM, total // 2), jnp.float32),
        ],
        compiler_params=pltpu.CompilerParams(vmem_limit_bytes=VMEM_LIMIT),
        cost_estimate=pl.CostEstimate(
            flops=total * total,
            bytes_accessed=HEAD_DIM * total,
            transcendentals=0,
        ),
    )(lengths, own, other, own_back, other_back, out, log_mass, cosine, sine)


TN = (((0,), (0,)), ((), ()))
PLAIN = (((1,), (0,)), ((), ()))
LANES = 128
GROUPS = 4
RUNS = 8
UNITS = FF // GROUPS
EXPAND_RUN = -(-2 * UNITS // (16 * RUNS)) * 16
SHRINK_RUN = -(-UNITS // (16 * RUNS)) * 16


def run_segments(start, stop, run):
    segments = []
    while start < stop:
        index = start // run
        end = min(stop, (index + 1) * run)
        segments.append((index, start - index * run, start, end - start))
        start = end
    return segments


def feed_kernel(
    second_ref,
    upstream_ref,
    active_ref,
    gate_ref,
    shrink_ref,
    shrunk_ref,
    second_back_ref,
    parts_ref,
    grads_ref,
    zero_ref,
    send_ref,
    zero_send_ref,
):
    index = pl.program_id(0)

    def joined(ref):
        return jnp.concatenate([ref[piece, 0] for piece in range(ref.shape[0])], axis=1)

    def product(left, right, dims):
        return lax.dot_general(left, right, dims, preferred_element_type=jnp.float32)

    def grad_copies(half, pair):
        moves = []
        for kind, member in ((0, pair), (1, pair + 2)):
            for run, place, offset, size in run_segments(
                half * UNITS, (half + 1) * UNITS, EXPAND_RUN
            ):
                moves.append((kind, offset - half * UNITS, run, member, place, size))
        for run, place, offset, size in run_segments(0, UNITS, SHRINK_RUN):
            moves.append((2, offset, run, 2 * pair + half, EXPAND_RUN + place, size))
        return [
            pltpu.make_async_copy(
                grads_ref.at[half, kind, pl.ds(offset, size), :],
                parts_ref.at[run, member, pl.ds(place, size), :],
                send_ref.at[half, number],
            )
            for number, (kind, offset, run, member, place, size) in enumerate(moves)
        ]

    def zero_copies():
        moves = []
        for member in range(GROUPS):
            for base, run_size, total in ((0, EXPAND_RUN, 2 * UNITS), (EXPAND_RUN, SHRINK_RUN, UNITS)):
                for run, place, _, size in run_segments(total, RUNS * run_size, run_size):
                    moves.append((run, member, base + place, size))
        return [
            pltpu.make_async_copy(
                zero_ref.at[pl.ds(0, size), :],
                parts_ref.at[run, member, pl.ds(place, size), :],
                zero_send_ref.at[number],
            )
            for number, (run, member, place, size) in enumerate(moves)
        ]

    @pl.when(index == 0)
    def fill():
        zero_ref[...] = jnp.zeros_like(zero_ref)
        for copy in zero_copies():
            copy.start()

    active, gate, shrink = joined(active_ref), joined(gate_ref), joined(shrink_ref)
    second, upstream = second_ref[...], upstream_ref[...]
    input_active = product(second, active, NT)
    input_gate = product(second, gate, NT)
    hidden_back = product(upstream, shrink, NT)
    below = 0.5 + 0.5 * lax.erf(input_active * 0.5**0.5)
    bell = jnp.exp(-0.5 * input_active * input_active) * (0.5 / math.pi) ** 0.5
    curve = input_active * below
    hidden = (curve * input_gate).astype(jnp.bfloat16)
    active_back = (hidden_back * input_gate * (below + input_active * bell)).astype(jnp.bfloat16)
    gate_back = (hidden_back * curve).astype(jnp.bfloat16)
    shrunk = product(hidden, shrink, PLAIN)
    second_back = product(active_back, active, PLAIN) + product(gate_back, gate, PLAIN)

    @pl.when(index == 0)
    def begin():
        shrunk_ref[...] = shrunk
        second_back_ref[...] = second_back

    @pl.when(index > 0)
    def add():
        shrunk_ref[...] += shrunk
        second_back_ref[...] += second_back

    for half in range(2):

        @pl.when(index % 2 == half)
        def send(half=half):
            pair = index // 2

            @pl.when(index >= 2)
            def free():
                for copy in grad_copies(half, pair - 1):
                    copy.wait()

            grads_ref[half, 0] = product(active_back, second, TN).astype(jnp.bfloat16)
            grads_ref[half, 1] = product(gate_back, second, TN).astype(jnp.bfloat16)
            grads_ref[half, 2] = product(hidden, upstream, TN).astype(jnp.bfloat16)
            for copy in grad_copies(half, pair):
                copy.start()

    @pl.when(index == GROUPS - 1)
    def drain():
        for half in range(2):
            for copy in grad_copies(half, 1):
                copy.wait()
        for copy in zero_copies():
            copy.wait()


def feed_forward(second, upstream, pieces):
    count, width = second.shape
    block = (RUNS, 1, UNITS, LANES)
    held = pl.BlockSpec((count, width), lambda i: (0, 0), pipeline_mode=pl.Buffered(1))
    wide = jax.ShapeDtypeStruct((count, width), jnp.float32)
    run = EXPAND_RUN + SHRINK_RUN
    copies = max(
        2 * len(run_segments(half * UNITS, (half + 1) * UNITS, EXPAND_RUN)) for half in range(2)
    ) + len(run_segments(0, UNITS, SHRINK_RUN))
    return pl.pallas_call(
        feed_kernel,
        grid=(GROUPS,),
        in_specs=[
            held,
            held,
            pl.BlockSpec(block, lambda i: (0, i // 2, i % 2, 0)),
            pl.BlockSpec(block, lambda i: (0, i // 2 + 2, i % 2, 0)),
            pl.BlockSpec(block, lambda i: (0, i, 2, 0)),
        ],
        out_specs=[held, held, pl.BlockSpec(memory_space=pl.ANY)],
        out_shape=[wide, wide, jax.ShapeDtypeStruct((RUNS, GROUPS, run, width), jnp.bfloat16)],
        scratch_shapes=[
            pltpu.VMEM((2, 3, UNITS, width), jnp.bfloat16),
            pltpu.VMEM((max(EXPAND_RUN, SHRINK_RUN), width), jnp.bfloat16),
            pltpu.SemaphoreType.DMA((2, copies)),
            pltpu.SemaphoreType.DMA((GROUPS * 8,)),
        ],
        compiler_params=pltpu.CompilerParams(vmem_limit_bytes=VMEM_LIMIT),
        cost_estimate=pl.CostEstimate(
            flops=count * width,
            bytes_accessed=count * width,
            transcendentals=0,
        ),
    )(second, upstream, pieces, pieces, pieces)


def enter_kernel(*refs):
    phases = (len(refs) - 9) // 2
    attend_refs, weight_refs = refs[:phases], refs[phases : 2 * phases]
    limit_ref, token_ref, cotangent_ref, gain_ref = refs[2 * phases : 2 * phases + 4]
    middle_ref, normal_ref, second_ref, upstream_ref, spread_ref = refs[2 * phases + 4 :]
    middle = token_ref[...].astype(jnp.float32)
    for attend_ref, weight_ref in zip(attend_refs, weight_refs):
        middle += lax.dot_general(
            attend_ref[...], weight_ref[...], TN, preferred_element_type=jnp.float32
        )
    block = middle.shape[0]
    centre = middle - jnp.mean(middle, axis=1, keepdims=True)
    scale = lax.rsqrt(jnp.mean(centre * centre, axis=1, keepdims=True) + NORM_EPS)
    normal = centre * scale
    place = pl.program_id(0) * block + lax.broadcasted_iota(jnp.int32, (block, 1), 0)
    middle_ref[...] = middle
    normal_ref[...] = normal
    spread_ref[...] = scale
    second_ref[...] = (normal * gain_ref[1:2, :]).astype(jnp.bfloat16)
    upstream_ref[...] = jnp.where(place < limit_ref[0], cotangent_ref[...], jnp.bfloat16(0.0))


def enter_feed(attends, weights, limit, tokens, cotangent, gains):
    count, width = tokens.shape
    block = min(256, count)
    rows = pl.BlockSpec((block, width), lambda i: (i, 0))
    wide = jax.ShapeDtypeStruct((count, width), jnp.float32)
    low = jax.ShapeDtypeStruct((count, width), jnp.bfloat16)
    return pl.pallas_call(
        enter_kernel,
        grid=(count // block,),
        in_specs=[pl.BlockSpec((attend.shape[0], block), lambda i: (0, i)) for attend in attends]
        + [pl.BlockSpec(weight.shape, lambda i: (0, 0)) for weight in weights]
        + [pl.BlockSpec(memory_space=pltpu.SMEM), rows, rows]
        + [pl.BlockSpec(gains.shape, lambda i: (0, 0))],
        out_specs=[rows, rows, rows, rows, pl.BlockSpec((block, 1), lambda i: (i, 0))],
        out_shape=[wide, wide, low, low, jax.ShapeDtypeStruct((count, 1), jnp.float32)],
        compiler_params=pltpu.CompilerParams(vmem_limit_bytes=VMEM_LIMIT),
        cost_estimate=pl.CostEstimate(
            flops=2 * count * width * width, bytes_accessed=20 * count * width, transcendentals=0
        ),
    )(*attends, *weights, limit, tokens, cotangent, gains)


def leave_kernel(*refs):
    phases = (len(refs) - 12) // 2
    weight_refs, back_refs = refs[:phases], refs[-phases:]
    limit_ref, shrunk_ref, change_ref, middle_ref, normal_ref, spread_ref = refs[phases : phases + 6]
    upstream_ref, gain_ref = refs[phases + 6 : phases + 8]
    mixed_ref, middle_back_ref, branch_ref, gain_grad_ref = refs[phases + 8 : phases + 12]
    index = pl.program_id(0)
    block = mixed_ref.shape[0]
    place = index * block + lax.broadcasted_iota(jnp.int32, (block, 1), 0)
    mixed = middle_ref[...] + shrunk_ref[...]
    mixed_ref[...] = jnp.where(place < limit_ref[0], mixed, 0.0).astype(jnp.bfloat16)
    change, normal = change_ref[...], normal_ref[...]
    gain_grad = jnp.sum(change * normal, axis=0, keepdims=True)

    @pl.when(index == 0)
    def begin():
        gain_grad_ref[...] = gain_grad

    @pl.when(index > 0)
    def add():
        gain_grad_ref[...] += gain_grad

    inner = change * gain_ref[1:2, :]
    inner = (
        inner
        - jnp.mean(inner, axis=1, keepdims=True)
        - normal * jnp.mean(inner * normal, axis=1, keepdims=True)
    )
    middle_back = upstream_ref[...].astype(jnp.float32) + spread_ref[...] * inner
    branch = middle_back.astype(jnp.bfloat16)
    middle_back_ref[...] = middle_back
    branch_ref[...] = branch
    for weight_ref, back_ref in zip(weight_refs, back_refs):
        back_ref[...] = lax.dot_general(
            weight_ref[...], branch, NT, preferred_element_type=jnp.float32
        ).astype(jnp.bfloat16)


def leave_feed(weights, limit, shrunk, change, middle, normal, spread, upstream, gains):
    count, width = shrunk.shape
    block = min(256, count)
    rows = pl.BlockSpec((block, width), lambda i: (i, 0))
    wide = jax.ShapeDtypeStruct((count, width), jnp.float32)
    low = jax.ShapeDtypeStruct((count, width), jnp.bfloat16)
    return pl.pallas_call(
        leave_kernel,
        grid=(count // block,),
        in_specs=[pl.BlockSpec(weight.shape, lambda i: (0, 0)) for weight in weights]
        + [pl.BlockSpec(memory_space=pltpu.SMEM), rows, rows, rows, rows]
        + [pl.BlockSpec((block, 1), lambda i: (i, 0)), rows]
        + [pl.BlockSpec(gains.shape, lambda i: (0, 0))],
        out_specs=[rows, rows, rows, pl.BlockSpec((1, width), lambda i: (0, 0))]
        + [pl.BlockSpec((weight.shape[0], block), lambda i: (0, i)) for weight in weights],
        out_shape=[low, wide, low, jax.ShapeDtypeStruct((1, width), jnp.float32)]
        + [jax.ShapeDtypeStruct((weight.shape[0], count), jnp.bfloat16) for weight in weights],
        compiler_params=pltpu.CompilerParams(vmem_limit_bytes=VMEM_LIMIT),
        cost_estimate=pl.CostEstimate(
            flops=2 * count * width * width, bytes_accessed=28 * count * width, transcendentals=0
        ),
    )(*weights, limit, shrunk, change, middle, normal, spread, upstream, gains)


def adam_step(rotated, first, second):
    average = BETA_ONE * first + (1.0 - BETA_ONE) * rotated
    variance = BETA_TWO * second + (1.0 - BETA_TWO) * rotated * rotated
    direction = (
        average / (1.0 - BETA_ONE**STEP) / (jnp.sqrt(variance / (1.0 - BETA_TWO**STEP)) + ADAM_EPS)
    )
    return (average, variance, direction)


def body(
    tokens,
    cotangent,
    lengths,
    triple_weight,
    output_weight,
    expand_weight,
    shrink_weight,
    norm_gains,
    side_bases,
    output_right,
    triple_first,
    triple_second,
    output_first,
    output_second,
    expand_first,
    expand_second,
    shrink_first,
    shrink_second,
    gains_first,
    gains_second,
):
    rows_here, local_len, width = tokens.shape
    count = rows_here * local_len
    shards = lax.axis_size("seq")
    groups = lax.axis_size("outer") * lax.axis_size("core")
    phases = HEADS // shards
    piece = width // shards
    fsdp = ("outer", "core")
    everyone = ("seq",) + fsdp
    offset = lax.axis_index("seq") * local_len
    position = offset + jnp.arange(local_len, dtype=jnp.int32)
    cosine, sine = rotary_tables(position)
    every = jnp.arange(shards * local_len, dtype=jnp.int32)
    all_cosine, all_sine = (
        table.reshape(HEAD_DIM // 2, shards, local_len).transpose(1, 0, 2)
        for table in rotary_tables(every)
    )
    valid = (position[None, :] < lengths[:, None]).astype(jnp.float32).reshape(count, 1)
    exchange = functools.partial(lax.all_to_all, axis_name="seq", split_axis=0, concat_axis=0)

    def tied(*values):
        return lax.optimization_barrier(values)

    def gathered(shard):
        flat = lax.all_gather(shard, everyone, axis=0, tiled=False)
        return flat.reshape((shards, groups) + shard.shape)

    triple_shards = (
        triple_weight.T.astype(jnp.bfloat16)
        .reshape(-1, phases, HEAD_DIM, piece)
        .transpose(1, 0, 2, 3)
        .reshape(phases, -1, piece)
    )
    triple_pieces = [gathered(triple_shards[0])]
    for phase in range(1, phases):
        shard, triple_pieces[-1] = tied(triple_shards[phase], triple_pieces[-1])
        triple_pieces.append(gathered(shard))
    output_columns = width // groups
    lanes = min(piece, output_columns)

    def fold(block):
        rows = block.shape[0]
        return block.reshape(rows, -1, lanes).transpose(1, 0, 2).reshape(-1, lanes)

    bases_low = side_bases.astype(jnp.bfloat16)
    right_low = output_right.astype(jnp.bfloat16)
    member = lax.axis_index("outer") * lax.axis_size("core") + lax.axis_index("core")
    base_rows = piece // groups
    flat = tokens.reshape(count, width).astype(jnp.float32)
    first_normed, first_back = jax.vjp(layer_norm, flat, norm_gains[0])
    first_low = first_normed.astype(jnp.bfloat16)
    projected = [
        project_heads(pieces, first_low, cosine, sine) for pieces in triple_pieces
    ]
    triple_rows = [rows for _, rows in projected]
    joints = [exchange(joint) for joint, _ in projected]
    other_shards = jnp.concatenate(
        [
            expand_weight.T.astype(jnp.bfloat16),
            shrink_weight.astype(jnp.bfloat16),
            fold(output_weight.astype(jnp.bfloat16)),
        ],
        axis=0,
    )
    other_shards, joints[0] = tied(other_shards, joints[0])
    other_pieces = gathered(other_shards)
    chosen = jnp.stack([bases_low[0], bases_low[2], bases_low[3]])
    chosen = lax.dynamic_slice_in_dim(chosen, member * base_rows, base_rows, 1)
    expand_rows = 2 * FF // groups
    shrink_rows = FF // groups
    output_rows = list(
        other_pieces[:, :, expand_rows + shrink_rows :]
        .reshape(shards, groups, output_columns // lanes, phases, HEAD_DIM, lanes)
        .transpose(3, 0, 4, 1, 2, 5)
        .reshape(phases, shards * HEAD_DIM, width)
    )
    canonical = (shards, groups, piece) == (RUNS, GROUPS, LANES)
    if canonical:
        feed_pieces = other_pieces
    else:
        feed_pieces = [
            other_pieces[:, :, start:end]
            .transpose(1, 2, 0, 3)
            .reshape(GROUPS, -1, RUNS, LANES)
            .transpose(2, 0, 1, 3)
            for start, end in ((0, expand_rows), (expand_rows, expand_rows + shrink_rows))
        ]
        feed_pieces = jnp.concatenate(feed_pieces, axis=2)
    swap = functools.partial(lax.ppermute, axis_name="core", perm=[(0, 1), (1, 0)])
    both_lengths = jnp.concatenate([lengths, swap(lengths)])
    others, forwards, attends = [], [], []
    for phase in range(phases):
        others.append(swap(joints[phase]))
        outcome = attend_forward(both_lengths, joints[phase], others[phase])
        if phase:
            attends[-1], outcome = tied(attends[-1], outcome)
        if phase < phases - 1:
            joints[phase + 1], outcome = tied(joints[phase + 1], outcome)
        forwards.append(outcome)
        attend = jnp.stack([outcome[0][0], swap(outcome[0][1])], axis=1)
        attends.append(exchange(attend.reshape(shards, HEAD_DIM, count)))
    chosen, forwards[-1] = tied(chosen, forwards[-1])
    bases_full = gathered(chosen)
    attends = [attend.reshape(shards * HEAD_DIM, count) for attend in attends]
    expand_height = -(-expand_rows // (16 * shards)) * 16
    shrink_height = -(-shrink_rows // (16 * shards)) * 16

    def to_rows(block):
        block = exchange(block)
        return block.transpose(1, 0, 2).reshape(block.shape[1], -1)

    def padded(block, height):
        block = jnp.pad(block, ((0, height * shards - block.shape[0]), (0, 0)))
        return block.reshape(shards, height, piece)

    def by_phase(block):
        return (
            block.reshape(-1, phases, HEAD_DIM, piece)
            .transpose(1, 0, 2, 3)
            .reshape(phases, shards, -1, piece)
        )

    def from_phases(blocks):
        block = jnp.stack(blocks).astype(jnp.float32).reshape(phases, -1, HEAD_DIM, piece)
        return block.transpose(1, 0, 2, 3).reshape(-1, piece)

    moments = []
    for expand, shrink, triple in (
        (expand_first, shrink_first, triple_first),
        (expand_second, shrink_second, triple_second),
    ):
        moments += [padded(expand.T, expand_height), padded(shrink, shrink_height)]
        moments += list(by_phase(triple.T))
    moments, attends[-1], feed_pieces = tied(moments, attends[-1], feed_pieces)
    heights = [moment.shape[1] for moment in moments]
    moments = to_rows(jnp.concatenate(moments, axis=1))
    edges = [sum(heights[:index]) for index in range(len(heights) + 1)]
    moments = [moments[start:end] for start, end in zip(edges, edges[1:])]
    moments = list(zip(moments[: phases + 2], moments[phases + 2 :]))
    inside = jnp.clip(lengths - offset, 0, local_len)
    middle, second_normal, second_low, upstream_low, second_spread = enter_feed(
        attends,
        output_rows,
        inside,
        tokens.reshape(count, width),
        cotangent.reshape(count, width),
        norm_gains,
    )
    shrunk, second_change, parts = feed_forward(second_low, upstream_low, feed_pieces)
    moments, bases_full, shrunk, second_change, parts = tied(
        moments, bases_full, shrunk, second_change, parts
    )
    bases_full = bases_full.transpose(2, 0, 1, 3, 4).reshape(3, width, width)
    mixed, middle_back, branch_low, second_gain, *backs = leave_feed(
        output_rows,
        inside,
        shrunk,
        second_change,
        middle,
        second_normal,
        second_spread,
        upstream_low,
        norm_gains,
    )
    mixed = mixed.reshape(tokens.shape)
    second_gain = second_gain[0]
    backs = [back.reshape(shards, HEAD_DIM, count) for back in backs]
    attend_backs = [exchange(back) for back in backs]

    def halved(blocks, axis, dim):
        size = lax.axis_size(axis)
        place = lax.axis_index(axis)
        while size > 1:
            size //= 2
            shape = blocks.shape
            blocks = blocks.reshape(shape[:dim] + (2, size) + shape[dim + 1 :])
            side = (place // size) % 2
            mine = lax.dynamic_index_in_dim(blocks, side, dim, keepdims=False)
            other = lax.dynamic_index_in_dim(blocks, 1 - side, dim, keepdims=False)
            pairs = [(member, member ^ size) for member in range(lax.axis_size(axis))]
            other = lax.ppermute(other, axis, pairs)
            blocks = (mine.astype(jnp.float32) + other.astype(jnp.float32)).astype(jnp.bfloat16)
        return jnp.squeeze(blocks, dim)

    def doubled(block, axis):
        block = block[None]
        place = lax.axis_index(axis)
        step = 1
        while step < lax.axis_size(axis):
            pairs = [(member, member ^ step) for member in range(lax.axis_size(axis))]
            other = lax.ppermute(block, axis, pairs)
            upper = (place // step) % 2 == 1
            block = jnp.concatenate(
                [jnp.where(upper, other, block), jnp.where(upper, block, other)], axis=0
            )
            step *= 2
        return block

    def near_sum(blocks):
        return halved(halved(blocks, "core", 1), "outer", 0)

    def merged(*blocks):
        sizes = [math.prod(block.shape[1:]) for block in blocks]
        flat = [block.reshape(shards, -1, piece) for block in blocks]
        flat = exchange(jnp.concatenate(flat, axis=1))
        results, start = [], 0
        for block, size in zip(blocks, sizes):
            rows = size // piece
            results.append(flat[:, start : start + rows].reshape(block.shape))
            start += rows
        return results

    def widened(block):
        rows = piece * output_columns // count
        block = block.reshape(-1, piece // rows, rows, output_columns)
        return block.swapaxes(1, 2).reshape(shards, -1, count)

    def narrowed(block):
        rows = piece * output_columns // count
        block = block.reshape(-1, rows, piece // rows, output_columns)
        return block.swapaxes(1, 2).reshape(shards, -1, piece, output_columns)

    def far_sum(terms):
        return jnp.sum(terms.astype(jnp.float32), axis=0).astype(jnp.bfloat16)

    def cut_rows(rows):
        return rows.reshape(rows.shape[0], shards, piece).transpose(1, 0, 2)

    outer = lax.axis_size("outer")
    output_part = jnp.stack(
        [
            jnp.dot(attend, branch_low, preferred_element_type=jnp.float32)
            .astype(jnp.bfloat16)
            .reshape(shards, HEAD_DIM, width)
            for attend in attends
        ],
        axis=1,
    )
    output_terms = halved(
        output_part.reshape(shards, piece, outer, -1, output_columns).transpose(0, 2, 3, 1, 4),
        "core",
        2,
    )
    def cut(product, height):
        block = product.reshape(groups, -1, width)
        block = jnp.pad(block, ((0, 0), (0, height * shards - block.shape[1]), (0, 0)))
        return block.reshape(groups, shards, height, width)

    if not canonical:
        parts = parts.transpose(1, 0, 2, 3)
        parts = [
            cut(block.reshape(GROUPS, -1, width)[:, : size // GROUPS], height)
            for block, size, height in (
                (parts[:, :, :EXPAND_RUN], 2 * FF, expand_height),
                (parts[:, :, EXPAND_RUN:], FF, shrink_height),
            )
        ]
        parts = jnp.concatenate(parts, axis=2).transpose(1, 0, 2, 3)
    parts = parts.reshape(shards * groups, -1, width)
    owned = lax.psum_scatter(parts, everyone, scatter_dimension=0, tiled=False)
    feed_height = expand_height + shrink_height

    def soap_rows(rows, base, moment):
        rotated = plain_product(rows, base)
        direction = adam_step(rotated, *moment)[2]
        step = back_product(direction.astype(jnp.bfloat16), base)
        return rotated.astype(jnp.bfloat16), step.astype(jnp.bfloat16)

    other_backs, grads = [], []
    for phase in range(phases):
        other_backs.append(swap(attend_backs[phase]))
        own_grad, other_grad = attend_backward(
            both_lengths,
            joints[phase],
            others[phase],
            attend_backs[phase],
            other_backs[phase],
            *forwards[phase],
            all_cosine,
            all_sine,
        )
        if phase < phases - 1:
            attend_backs[phase + 1], output_terms, own_grad, other_grad = tied(
                attend_backs[phase + 1], output_terms, own_grad, other_grad
            )
        else:
            grads, owned, own_grad, other_grad = tied(grads, owned, own_grad, other_grad)
        grad = own_grad.astype(jnp.float32) + swap(other_grad).astype(jnp.float32)
        grad = grad.astype(jnp.bfloat16)
        if phase == 0:
            grad = jnp.concatenate([grad, widened(output_terms)], axis=1)
        grads.append(exchange(grad))
    output_low = halved(far_sum(narrowed(grads[0][:, 3 * HEAD_DIM :])), "outer", 0)
    grads[0] = grads[0][:, : 3 * HEAD_DIM]
    output_left = outer_sum(bases_low[1], output_low).astype(jnp.bfloat16)
    output_left = output_left.reshape(shards, piece, output_columns)

    def triple_sum(grad):
        joint_back = grad.reshape(shards * 3 * HEAD_DIM, count)
        part = jnp.dot(joint_back, first_low, preferred_element_type=jnp.float32)
        part = part.astype(jnp.bfloat16).reshape(shards, 3, HEAD_DIM, width).swapaxes(0, 1)
        return near_sum(part.reshape(outer, groups // outer, shards, -1, width)), joint_back

    def triple_rest(terms, phase):
        rows = far_sum(terms)
        return jnp.concatenate([rows, *soap_rows(rows, bases_full[0], moments[2 + phase])])

    last = phases - 1
    summed = [triple_sum(grads[phase]) for phase in range(last)]
    feed_rows = jnp.concatenate(
        [
            owned,
            *soap_rows(owned[:expand_height], bases_full[1], moments[0]),
            *soap_rows(owned[expand_height:], bases_full[2], moments[1]),
        ]
    )
    grads[last], summed, feed_rows, output_left = tied(
        grads[last], summed, feed_rows, output_left
    )
    settled, output_left = merged(cut_rows(feed_rows), output_left)
    output_left = far_sum(output_left)
    summed.append(triple_sum(grads[last]))
    joint_backs = [joint_back for _, joint_back in summed]
    terms = exchange(jnp.concatenate([term for term, _ in summed], axis=1))
    terms = jnp.split(terms, phases, axis=1)
    triple_done = [triple_rest(term, phase) for phase, term in enumerate(terms)]
    output_turned = plain_product(output_left, right_low).astype(jnp.bfloat16)
    output_turned = near_sum(
        output_turned.reshape(piece, outer, -1, output_columns).transpose(1, 2, 0, 3)
    ).astype(jnp.float32)
    output_average, output_variance, output_direction = adam_step(
        output_turned, output_first, output_second
    )
    output_wide = doubled(doubled(output_direction.astype(jnp.bfloat16), "core"), "outer")
    output_wide = output_wide.reshape(groups, piece, output_columns).swapaxes(0, 1)
    output_middle = back_product(output_wide.reshape(piece, width), right_low)
    *triple_done, output_middle = merged(
        *[cut_rows(rows) for rows in triple_done],
        jnp.broadcast_to(output_middle.astype(jnp.bfloat16), (shards, piece, output_columns)),
    )
    output_back = plain_product(bases_low[1], output_middle.reshape(width, output_columns))
    triple_lows, triple_turns, triple_steps = zip(
        *[jnp.split(done, 3, axis=1) for done in triple_done]
    )

    def settled_piece(start, height, size):
        return settled[:, start : start + height].reshape(-1, piece)[:size].astype(jnp.float32)

    expand_gradient, expand_turned_grad, expand_back = (
        settled_piece(start, expand_height, expand_rows).T
        for start in (0, feed_height, feed_height + expand_height)
    )
    shrink_gradient, shrink_turned_grad, shrink_back = (
        settled_piece(start, shrink_height, shrink_rows)
        for start in (
            expand_height,
            feed_height + 2 * expand_height,
            feed_height + 2 * expand_height + shrink_height,
        )
    )
    expand_average, expand_variance, _ = adam_step(expand_turned_grad, expand_first, expand_second)
    shrink_average, shrink_variance, _ = adam_step(shrink_turned_grad, shrink_first, shrink_second)
    triple_turned = from_phases(triple_turns).T
    triple_back = from_phases(triple_steps).T
    triple_gradient = from_phases(triple_lows).T
    triple_average, triple_variance, _ = adam_step(triple_turned, triple_first, triple_second)
    first_input, first_gain = first_back(
        sum(
            outer_sum(joint_back, rows.reshape(-1, width))
            for joint_back, rows in zip(joint_backs, triple_rows)
        )
    )
    token_gradient = (middle_back + first_input).astype(jnp.bfloat16).reshape(tokens.shape)
    gains_gradient = jnp.stack([first_gain, second_gain])
    for axis in ("core", "outer", "seq"):
        members = range(lax.axis_size(axis))
        for step in range(len(members).bit_length() - 1):
            pairs = [(member, member ^ (1 << step)) for member in members]
            gains_gradient = gains_gradient + lax.ppermute(gains_gradient, axis, pairs)
    gains_average, gains_variance, gains_direction = adam_step(
        gains_gradient, gains_first, gains_second
    )
    output_gradient = output_low.astype(jnp.float32)
    triple_updated = (triple_weight - WEIGHT_RATES[0] * triple_back) * (
        1.0 - WEIGHT_RATES[0] * DECAY_RATE
    )
    output_updated = (output_weight - WEIGHT_RATES[1] * output_back) * (
        1.0 - WEIGHT_RATES[1] * DECAY_RATE
    )
    expand_updated = (expand_weight - WEIGHT_RATES[2] * expand_back) * (
        1.0 - WEIGHT_RATES[2] * DECAY_RATE
    )
    shrink_updated = (shrink_weight - WEIGHT_RATES[3] * shrink_back) * (
        1.0 - WEIGHT_RATES[3] * DECAY_RATE
    )
    gains_updated = norm_gains - GAINS_RATE * gains_direction
    return (
        mixed,
        token_gradient,
        triple_gradient,
        output_gradient,
        expand_gradient,
        shrink_gradient,
        gains_gradient,
        triple_average,
        triple_variance,
        triple_updated,
        triple_updated.astype(jnp.bfloat16),
        output_average,
        output_variance,
        output_updated,
        output_updated.astype(jnp.bfloat16),
        expand_average,
        expand_variance,
        expand_updated,
        expand_updated.astype(jnp.bfloat16),
        shrink_average,
        shrink_variance,
        shrink_updated,
        shrink_updated.astype(jnp.bfloat16),
        gains_average,
        gains_variance,
        gains_updated,
    )


def solution(mesh):
    in_specs = (
        P(("outer", "core"), "seq", None),
        P(("outer", "core"), "seq", None),
        P(("outer", "core")),
        P("seq", ("outer", "core")),
        P("seq", ("outer", "core")),
        P("seq", ("outer", "core")),
        P(("outer", "core"), "seq"),
        P(),
        P(None, "seq", None),
        P(("outer", "core"), None),
        P("seq", ("outer", "core")),
        P("seq", ("outer", "core")),
        P("seq", ("outer", "core")),
        P("seq", ("outer", "core")),
        P("seq", ("outer", "core")),
        P("seq", ("outer", "core")),
        P(("outer", "core"), "seq"),
        P(("outer", "core"), "seq"),
        P(),
        P(),
    )
    out_specs = (
        P(("outer", "core"), "seq", None),
        P(("outer", "core"), "seq", None),
        P("seq", ("outer", "core")),
        P("seq", ("outer", "core")),
        P("seq", ("outer", "core")),
        P(("outer", "core"), "seq"),
        P(),
        P("seq", ("outer", "core")),
        P("seq", ("outer", "core")),
        P("seq", ("outer", "core")),
        P("seq", ("outer", "core")),
        P("seq", ("outer", "core")),
        P("seq", ("outer", "core")),
        P("seq", ("outer", "core")),
        P("seq", ("outer", "core")),
        P("seq", ("outer", "core")),
        P("seq", ("outer", "core")),
        P("seq", ("outer", "core")),
        P("seq", ("outer", "core")),
        P(("outer", "core"), "seq"),
        P(("outer", "core"), "seq"),
        P(("outer", "core"), "seq"),
        P(("outer", "core"), "seq"),
        P(),
        P(),
        P(),
    )
    groups = mesh.shape["fsdp"]
    devices = mesh.devices.reshape(mesh.shape["seq"], groups // 2, 2)
    split = Mesh(devices, ("seq", "outer", "core"))
    return jax.shard_map(body, mesh=split, in_specs=in_specs, out_specs=out_specs, check_vma=False)
```

profile of v0, /device:TPU:0, one launch (start us, length us, event | category | flops | bytes accessed | tf_op | source)
XLA Modules:
  0.0 1168.3 jit_solution(7469641866656275393)
XLA Ops:
  14.1 59.2 %all-gather.8.cloned.1.call-done = bf16[32,384,128]{2,1,0:T(8,128)(2,1)} async-done(((bf16[1,384,128]{2,1,0:T(8,128)(2,1)}), bf16[32,384,128]{2,1,0:T(8,128)(2,1)}) %all-gather.8.cloned.1.call-update) | async-done | bytes 3145744 | tf_op jit(solution)/shard_map/all_gather | solution.py:744
  75.3 7.1 shard_map.395
  82.5 4.4 all-to-all-start
  89.9 82.2 %all-to-all-done.own_ref = bf16[8,192,1024]{2,1,0:T(8,128)(2,1)S(1)} async-done(((bf16[8,192,1024]{2,1,0:T(8,128)(2,1)}), bf16[8,192,1024]{2,1,0:T(8,128)(2,1)S(1)}, u32[]{:S(2)}, u32[]{:S(2)}) %all-to-all-start) | async-done | bytes 3145760 | tf_op jit(solution)/shard_map/all_to_all | solution.py:775
  173.4 7.1 shard_map.396
  180.6 4.0 all-to-all-start.1
  185.7 4.8 collective-permute-done
  191.7 32.0 %shard_map.397 = (bf16[2,4,64,1024]{3,2,1,0:T(8,128)(2,1)}, f32[2,4,1,1024]{3,2,1,0:T(1,128)}) custom-call(s32[2]{0:T(128)} %pad_add_fusion.length_ref, bf16[8,192,1024]{2,1,0:T(8,128)(2,1)} %copy-done.4, bf16[8,192,1024]{2,1,0:T(8,128)(2,1)} %collective-permute-done.1.other_ref), custom_call_target="tpu_custom_call" | custom-call | flops 67108864 | bytes 524288 | tf_op jit(solution)/shard_map/pallas_call | solution.py:243
  223.7 68.6 %all-to-all-done.1.own_ref = bf16[8,192,1024]{2,1,0:T(8,128)(2,1)S(1)} async-done(((bf16[8,192,1024]{2,1,0:T(8,128)(2,1)}), bf16[8,192,1024]{2,1,0:T(8,128)(2,1)S(1)}, u32[]{:S(2)}, u32[]{:S(2)}) %all-to-all-start.1) | async-done | bytes 3145760 | tf_op jit(solution)/shard_map/all_to_all | solution.py:775
  294.8 3.2 collective-permute-done.2
  299.1 5.1 all-to-all-start.2
  309.2 32.0 %shard_map.398 = (bf16[2,4,64,1024]{3,2,1,0:T(8,128)(2,1)}, f32[2,4,1,1024]{3,2,1,0:T(1,128)}) custom-call(s32[2]{0:T(128)} %pad_add_fusion.length_ref, bf16[8,192,1024]{2,1,0:T(8,128)(2,1)} %copy-done.3, bf16[8,192,1024]{2,1,0:T(8,128)(2,1)} %collective-permute-done.3.other_ref), custom_call_target="tpu_custom_call" | custom-call | flops 67108864 | bytes 524288 | tf_op jit(solution)/shard_map/pallas_call | solution.py:243
  341.1 17.6 %all-to-all-done.2 = bf16[8,64,1024]{2,1,0:T(8,128)(2,1)} async-done(((bf16[8,64,1024]{2,1,0:T(8,128)(2,1)}), bf16[8,64,1024]{2,1,0:T(8,128)(2,1)}, u32[]{:S(2)}, u32[]{:S(2)}) %all-to-all-start.2) | async-done | bytes 1048608 | tf_op jit(solution)/shard_map/all_to_all | solution.py:820
  363.3 5.9 all-to-all-start.3
  375.8 23.6 %all-to-all-done.3 = bf16[8,64,1024]{2,1,0:T(8,128)(2,1)S(1)} async-done(((bf16[8,64,1024]{2,1,0:T(8,128)(2,1)}), bf16[8,64,1024]{2,1,0:T(8,128)(2,1)S(1)}, u32[]{:S(2)}, u32[]{:S(2)}) %all-to-all-start.3) | async-done | bytes 1048608 | tf_op jit(solution)/shard_map/all_to_all | solution.py:820
  408.6 3.6 all-to-all-start.4
  416.2 2.5 fusion.126
  418.7 2.6 unstack.37.refs_2_.refs_0_
  421.2 2.6 unstack.39.refs_3_.refs_1_
  423.8 9.4 shard_map.399
  433.3 81.5 %shard_map.400 = (f32[1024,1024]{1,0:T(8,128)}, f32[1024,1024]{1,0:T(8,128)}, bf16[8,4,272,1024]{3,2,1,0:T(8,128)(2,1)}) custom-call(bf16[1024,1024]{1,0:T(8,128)(2,1)} %get-tuple-element.125.second_ref, bf16[1024,1024]{1,0:T(8,128)(2,1)} %get-tuple-element.126.upstream_ref.refs_8_, bf16[8,4,2224,128]{3,2,1,0:T(8,128)(2,1)} %bitcast.336, ...), custom_call_target="tpu_custom_call" | custom-call | flops 1048576 | bytes 1048576 | tf_op jit(solution)/shard_map/pallas_call | solution.py:557
  518.8 12.6 %shard_map.401 = (bf16[1024,1024]{1,0:T(8,128)(2,1)}, f32[1024,1024]{1,0:T(8,128)}, bf16[1024,1024]{1,0:T(8,128)(2,1)}, f32[1,1024]{1,0:T(1,128)}, bf16[512,1024]{1,0:T(8,128)(2,1)}, /*index=5*/bf16[512,1024]{1,0:T(8,128)(2,1)}) custom-call(bf16[512,1024]{1,0:T(8,128)(2,1)} %unstack.37.refs_2_.refs_0_, bf16[512,1024]{1,0:T(8,128)(2,1)} %unstack.39.refs_3_.refs_1_, ...), custom_call_target="tpu_custom_call" | custom-call | flops 2147483648 | bytes 29360128 | tf_op jit(solution)/shard_map/pallas_call | solution.py:672
  531.4 5.9 all-to-all-start.6
  537.3 3.3 convolution_convert_fusion.3
  542.0 28.3 %all-to-all-done.6.own_back_ref = bf16[8,64,1024]{2,1,0:T(8,128)(2,1)S(1)} async-done(((bf16[8,64,1024]{2,1,0:T(8,128)(2,1)}), bf16[8,64,1024]{2,1,0:T(8,128)(2,1)S(1)}, u32[]{:S(2)}, u32[]{:S(2)}) %all-to-all-start.6) | async-done | bytes 1048608 | tf_op jit(solution)/shard_map/all_to_all | solution.py:887
  570.3 7.7 all-to-all-start.5
  579.4 3.3 reshape.490
  582.7 4.9 constant_dynamic-slice_fusion.3
  588.4 4.8 multiply_sine_fusion
  594.6 80.2 %shard_map.402 = (bf16[8,192,1024]{2,1,0:T(8,128)(2,1)}, bf16[8,192,1024]{2,1,0:T(8,128)(2,1)}) custom-call(s32[2]{0:T(128)} %pad_add_fusion.length_ref, bf16[8,192,1024]{2,1,0:T(8,128)(2,1)} %copy-done.4, bf16[8,192,1024]{2,1,0:T(8,128)(2,1)} %collective-permute-done.1.other_ref, bf16[8,64,1024]{2,1,0:T(8,128)(2,1)} %copy-done.16, ...), custom_call_target="tpu_custom_call" | custom-call | flops 67108864 | bytes 524288 | tf_op jit(solution)/shard_map/pallas_call | solution.py:391
  676.6 4.2 collective-permute-done.7
  680.9 4.6 add_convert_fusion.1
  685.5 2.8 pad_maximum_fusion
  688.3 6.2 all-to-all-start.7
  694.6 2.9 collective-permute-done.8.other_back_ref
  698.4 80.7 %shard_map.403 = (bf16[8,192,1024]{2,1,0:T(8,128)(2,1)}, bf16[8,192,1024]{2,1,0:T(8,128)(2,1)}) custom-call(s32[2]{0:T(128)} %pad_add_fusion.length_ref, bf16[8,192,1024]{2,1,0:T(8,128)(2,1)} %copy-done.3, bf16[8,192,1024]{2,1,0:T(8,128)(2,1)} %collective-permute-done.3.other_ref, bf16[8,64,1024]{2,1,0:T(8,128)(2,1)} %all-to-all-done.5.own_back_ref, ...), custom_call_target="tpu_custom_call" | custom-call | flops 67108864 | bytes 524288 | tf_op jit(solution)/shard_map/pallas_call | solution.py:391
  779.1 31.1 %all-to-all-done.7 = bf16[8,256,1024]{2,1,0:T(8,128)(2,1)} async-done(((bf16[8,256,1024]{2,1,0:T(8,128)(2,1)}), bf16[8,256,1024]{2,1,0:T(8,128)(2,1)}, u32[]{:S(2)}, u32[]{:S(2)}) %all-to-all-start.7) | async-done | bytes 4194336 | tf_op jit(solution)/shard_map/all_to_all | solution.py:1011
  810.2 5.9 collective-permute-done.9
  816.1 5.2 add_convert_fusion
  821.3 17.7 %all-to-all-start.8 = ((bf16[8,192,1024]{2,1,0:T(8,128)(2,1)}), bf16[8,192,1024]{2,1,0:T(8,128)(2,1)}, u32[]{:S(2)}, u32[]{:S(2)}) async-start(bf16[8,192,1024]{2,1,0:T(8,128)(2,1)} %add_convert_fusion), calls=%async_computation.9 | async-start | bytes 6291456 | tf_op jit(solution)/shard_map/all_to_all | solution.py:1011
  839.0 2.3 slice.203
  841.5 3.9 convolution_convert_fusion.1
  848.9 5.9 fusion.123
  861.0 91.8 %collective-permute-start.12 = (bf16[1,128,256]{2,1,0:T(8,128)(2,1)S(1)}, bf16[1,128,256]{2,1,0:T(8,128)(2,1)S(1)}, u32[]{:S(2)}, u32[]{:S(2)}) collective-permute-start(bf16[1,128,256]{2,1,0:T(8,128)(2,1)S(1)} %constant_dynamic-slice_fusion.2), channel_id=1, source_target_pairs={{0,2},{2,0},{1,3},{3,1},{4,6},{6,4},{5,7},{7,5},{8,10},{10,8},{9,1... | collective-permute-start | bytes 196616 | tf_op jit(solution)/shard_map/ppermute | solution.py:900
  953.9 2.3 convert_dynamic-update-slice_fusion
  965.1 13.1 %collective-permute-done.11 = bf16[1,8,48,1024]{3,2,1,0:T(8,128)(2,1)S(1)} collective-permute-done((bf16[1,8,48,1024]{3,2,1,0:T(8,128)(2,1)S(1)}, bf16[1,8,48,1024]{3,2,1,0:T(8,128)(2,1)S(1)}, u32[]{:S(2)}, u32[]{:S(2)}) %collective-permute-start.11) | collective-permute-done | bytes 786464 | tf_op jit(solution)/shard_map/ppermute | solution.py:900
  979.5 5.8 convolution_convert_fusion
  994.4 3.1 pad_maximum_fusion.1
  997.5 6.3 all-to-all-start.10
  1003.8 6.5 fusion.134
  1010.2 6.2 fusion.9
  1016.5 3.0 fusion.7
  1022.7 21.1 %collective-permute-start.20 = (f32[2,1024]{1,0:T(2,128)S(1)}, f32[2,1024]{1,0:T(2,128)S(1)}, u32[]{:S(2)}, u32[]{:S(2)}) collective-permute-start(f32[2,1024]{1,0:T(2,128)S(1)} %fusion.112), channel_id=1, source_target_pairs={{0,2},{2,0},{1,3},{3,1},{4,6},{6,4},{5,7},{7,5},{8,10},{10,8},{9,1... | collective-permute-start | bytes 24584 | tf_op jit(solution)/shard_map/ppermute | solution.py:1098
  1048.0 2.6 fusion.10
  1054.3 4.3 fusion.13
  1058.6 2.5 collective-permute-start.23
  1061.0 8.8 collective-permute-done.14
  1071.4 5.2 all-to-all-start.9
  1080.3 4.0 collective-permute-start.16
  1092.3 3.3 collective-permute-done.18
  1098.2 2.3 convolution_convert_fusion.10
  1101.9 10.8 all-to-all-done.9
  1118.3 3.7 all-to-all-start.11
  1130.0 19.1 %all-to-all-done.11 = bf16[8,544,128]{2,1,0:T(8,128)(2,1)S(1)} async-done(((bf16[8,544,128]{2,1,0:T(8,128)(2,1)}), bf16[8,544,128]{2,1,0:T(8,128)(2,1)S(1)}, u32[]{:S(2)}, u32[]{:S(2)}) %all-to-all-start.11) | async-done | bytes 1114144 | tf_op jit(solution)/shard_map/all_to_all | solution.py:924
  (334 shorter events, 143.0 us)
Async XLA Ops:
  7.2 66.1 %all-gather.8.cloned.1.call-start = ((), (), s32[]{:S(2)}) async-start(), calls=%async_computation.13 | async-start | bytes 3244032 | tf_op jit(solution)/shard_map/all_gather | solution.py:744
  8.6 66.8 %copy-start.18 = (f32[128,768]{0,1:T(8,128)}, f32[128,768]{0,1:T(8,128)S(1)}, u32[]{:S(2)}) copy-start(f32[128,768]{0,1:T(8,128)S(1)} %copy.160) | copy-start | bytes 1179652
  9.4 164.0 %all-gather.12.cloned.1.call-start = ((), (), s32[]{:S(2)}) async-start(), calls=%async_computation.16 | async-start | bytes 3244032 | tf_op jit(solution)/shard_map/all_gather | solution.py:744
  10.2 65.2 %copy-start.64 = (f32[32]{0:T(128)}, f32[32]{0:T(128)S(1)}, u32[]{:S(2)}) copy-start(f32[32]{0:T(128)S(1)} %multiply_power_fusion) | copy-start | bytes 388
  82.5 89.6 %all-to-all-start = ((bf16[8,192,1024]{2,1,0:T(8,128)(2,1)}), bf16[8,192,1024]{2,1,0:T(8,128)(2,1)S(1)}, u32[]{:S(2)}, u32[]{:S(2)}) async-start(bf16[8,192,1024]{2,1,0:T(8,128)(2,1)} %get-tuple-element.101), calls=%async_computation | async-start | bytes 6291456 | tf_op jit(solution)/shard_map/all_to_all | solution.py:775
  86.9 312.5 %all-gather.10.cloned.1.call-start = ((), (), s32[]{:S(2)}) async-start(), calls=%async_computation.15 | async-start | bytes 18788352 | tf_op jit(solution)/shard_map/all_gather | solution.py:744
  172.0 8.5 copy-start.4
  180.6 111.7 %all-to-all-start.1 = ((bf16[8,192,1024]{2,1,0:T(8,128)(2,1)}), bf16[8,192,1024]{2,1,0:T(8,128)(2,1)S(1)}, u32[]{:S(2)}, u32[]{:S(2)}) async-start(bf16[8,192,1024]{2,1,0:T(8,128)(2,1)} %get-tuple-element.104), calls=%async_computation.1 | async-start | bytes 6291456 | tf_op jit(solution)/shard_map/all_to_all | solution.py:775
  184.6 7.2 collective-permute-start.1
  184.6 6.0 collective-permute-start
  292.3 16.9 %collective-permute-start.3 = (bf16[8,192,1024]{2,1,0:T(8,128)(2,1)S(1)}, bf16[8,192,1024]{2,1,0:T(8,128)(2,1)}, u32[]{:S(2)}, u32[]{:S(2)}) collective-permute-start(bf16[8,192,1024]{2,1,0:T(8,128)(2,1)S(1)} %all-to-all-done.1.own_ref), channel_id=1, source_target_pairs={{0,1},{1,0},{2,3},{3,2},{4,5},{5,4},{6,7},{7,6},{8,9},{9,8},{10,11... | collective-permute-start | bytes 9437192 | tf_op jit(solution)/shard_map/ppermute | solution.py:812
  294.5 3.5 collective-permute-start.2
  299.1 59.6 %all-to-all-start.2 = ((bf16[8,64,1024]{2,1,0:T(8,128)(2,1)}), bf16[8,64,1024]{2,1,0:T(8,128)(2,1)}, u32[]{:S(2)}, u32[]{:S(2)}) async-start(bf16[8,64,1024]{2,1,0:T(8,128)(2,1)} %bitcast.361), calls=%async_computation.2 | async-start | bytes 2097152 | tf_op jit(solution)/shard_map/all_to_all | solution.py:820
  304.2 214.6 %all-gather.14.cloned.1.call-start = ((), (), s32[]{:S(2)}) async-start(), calls=%async_computation.17 | async-start | bytes 6488064 | tf_op jit(solution)/shard_map/all_gather | solution.py:744
  360.1 2.0 collective-permute-start.4
  363.3 36.1 %all-to-all-start.3 = ((bf16[8,64,1024]{2,1,0:T(8,128)(2,1)}), bf16[8,64,1024]{2,1,0:T(8,128)(2,1)S(1)}, u32[]{:S(2)}, u32[]{:S(2)}) async-start(bf16[8,64,1024]{2,1,0:T(8,128)(2,1)} %bitcast.46), calls=%async_computation.3 | async-start | bytes 2097152 | tf_op jit(solution)/shard_map/all_to_all | solution.py:820
  369.5 30.9 %copy-start.20 = (f32[128,768]{0,1:T(8,128)}, f32[128,768]{0,1:T(8,128)S(1)}, u32[]{:S(2)}) copy-start(f32[128,768]{0,1:T(8,128)S(1)} %copy.163) | copy-start | bytes 1179652
  399.4 9.2 copy-start.14
  399.4 7.8 copy-start.38
  408.6 106.1 %all-to-all-start.4 = ((f32[8,736,128]{2,1,0:T(8,128)}), f32[8,736,128]{2,1,0:T(8,128)S(1)}, u32[]{:S(2)}, u32[]{:S(2)}) async-start(f32[8,736,128]{2,1,0:T(8,128)} %constant_dynamic-update-slice_fusion), calls=%async_computation.4 | async-start | bytes 6029312 | tf_op jit(solution)/shard_map/all_to_all | solution.py:828
  412.2 398.0 %reduce-scatter.2.cloned.1.call-start = ((), (), s32[]{:S(2)}) async-start(), calls=%async_computation.14 | async-start | bytes 18382848 | tf_op jit(solution)/shard_map/reduce_scatter | solution.py:979
  531.4 38.8 %all-to-all-start.6 = ((bf16[8,64,1024]{2,1,0:T(8,128)(2,1)}), bf16[8,64,1024]{2,1,0:T(8,128)(2,1)S(1)}, u32[]{:S(2)}, u32[]{:S(2)}) async-start(bf16[8,64,1024]{2,1,0:T(8,128)(2,1)} %bitcast.385), calls=%async_computation.6 | async-start | bytes 2097152 | tf_op jit(solution)/shard_map/all_to_all | solution.py:887
  570.3 17.7 %copy-start.16 = (bf16[8,64,1024]{2,1,0:T(8,128)(2,1)}, bf16[8,64,1024]{2,1,0:T(8,128)(2,1)S(1)}, u32[]{:S(2)}) copy-start(bf16[8,64,1024]{2,1,0:T(8,128)(2,1)S(1)} %all-to-all-done.6.own_back_ref) | copy-start | bytes 3145732
  570.3 104.6 %all-to-all-start.5 = ((bf16[8,64,1024]{2,1,0:T(8,128)(2,1)}), bf16[8,64,1024]{2,1,0:T(8,128)(2,1)}, u32[]{:S(2)}, u32[]{:S(2)}) async-start(bf16[8,64,1024]{2,1,0:T(8,128)(2,1)} %bitcast.53), calls=%async_computation.5 | async-start | bytes 2097152 | tf_op jit(solution)/shard_map/all_to_all | solution.py:887
  587.8 5.4 collective-permute-start.5
  587.9 5.7 collective-permute-start.6
  674.9 6.0 collective-permute-start.7
  688.3 121.9 %all-to-all-start.7 = ((bf16[8,256,1024]{2,1,0:T(8,128)(2,1)}), bf16[8,256,1024]{2,1,0:T(8,128)(2,1)}, u32[]{:S(2)}, u32[]{:S(2)}) async-start(bf16[8,256,1024]{2,1,0:T(8,128)(2,1)} %pad_maximum_fusion), calls=%async_computation.7 | async-start | bytes 8388608 | tf_op jit(solution)/shard_map/all_to_all | solution.py:1011
  694.6 2.9 collective-permute-start.8
  810.2 5.9 collective-permute-start.9
  821.3 158.2 %all-to-all-start.8 = ((bf16[8,192,1024]{2,1,0:T(8,128)(2,1)}), bf16[8,192,1024]{2,1,0:T(8,128)(2,1)}, u32[]{:S(2)}, u32[]{:S(2)}) async-start(bf16[8,192,1024]{2,1,0:T(8,128)(2,1)} %add_convert_fusion), calls=%async_computation.9 | async-start | bytes 6291456 | tf_op jit(solution)/shard_map/all_to_all | solution.py:1011
  848.9 107.3 %collective-permute-start.10 = (bf16[2,1,8,48,1024]{4,3,2,0,1:T(8,128)(2,1)}, bf16[2,1,8,48,1024]{4,3,2,0,1:T(8,128)(2,1)}, u32[]{:S(2)}, u32[]{:S(2)}) collective-permute-start(bf16[2,1,8,48,1024]{4,3,2,0,1:T(8,128)(2,1)} %dynamic-slice_bitcast_fusion.2), channel_id=1, source_target_pairs={{0,1},{1,0},{2,3},{3,2},{4,5},{5,4},{6,7},{7,6},{8,9},{9,8},{10,11... | collective-permute-start | bytes 4718600 | tf_op jit(solution)/shard_map/ppermute | solution.py:900
  860.0 96.2 %copy-start.9 = (bf16[8,3,64,1024]{3,2,0,1:T(8,128)(2,1)S(1)}, bf16[8,3,64,1024]{3,2,0,1:T(8,128)(2,1)}, u32[]{:S(2)}) copy-start(bf16[8,3,64,1024]{3,2,0,1:T(8,128)(2,1)} %copy-done.8) | copy-start | bytes 9437188
  861.0 102.9 %collective-permute-start.12 = (bf16[1,128,256]{2,1,0:T(8,128)(2,1)S(1)}, bf16[1,128,256]{2,1,0:T(8,128)(2,1)S(1)}, u32[]{:S(2)}, u32[]{:S(2)}) collective-permute-start(bf16[1,128,256]{2,1,0:T(8,128)(2,1)S(1)} %constant_dynamic-slice_fusion.2), channel_id=1, source_target_pairs={{0,2},{2,0},{1,3},{3,1},{4,6},{6,4},{5,7},{7,5},{8,10},{10,8},{9,1... | collective-permute-start | bytes 196616 | tf_op jit(solution)/shard_map/ppermute | solution.py:900
  958.5 19.7 %collective-permute-start.11 = (bf16[1,8,48,1024]{3,2,1,0:T(8,128)(2,1)S(1)}, bf16[1,8,48,1024]{3,2,1,0:T(8,128)(2,1)S(1)}, u32[]{:S(2)}, u32[]{:S(2)}) collective-permute-start(bf16[1,8,48,1024]{3,2,1,0:T(8,128)(2,1)S(1)} %dynamic-slice_bitcast_fusion.4), channel_id=1, source_target_pairs={{0,2},{2,0},{1,3},{3,1},{4,6},{6,4},{5,7},{7,5},{8,10},{10,8},{9,1... | collective-permute-start | bytes 2359304 | tf_op jit(solution)/shard_map/ppermute | solution.py:900
  963.9 14.4 %copy-start.54 = (bf16[1,128,256]{2,1,0:T(8,128)(2,1)}, bf16[1,128,256]{2,1,0:T(8,128)(2,1)S(1)}, u32[]{:S(2)}) copy-start(bf16[1,128,256]{2,1,0:T(8,128)(2,1)S(1)} %collective-permute-done.12) | copy-start | bytes 196612
  988.8 59.2 %collective-permute-start.13 = (bf16[2,1,8,48,1024]{4,3,2,1,0:T(8,128)(2,1)}, bf16[2,1,8,48,1024]{4,3,2,1,0:T(8,128)(2,1)}, u32[]{:S(2)}, u32[]{:S(2)}) collective-permute-start(bf16[2,1,8,48,1024]{4,3,2,1,0:T(8,128)(2,1)} %dynamic-slice_bitcast_fusion.1), channel_id=1, source_target_pairs={{0,1},{1,0},{2,3},{3,2},{4,5},{5,4},{6,7},{7,6},{8,9},{9,8},{10,11... | collective-permute-start | bytes 4718600 | tf_op jit(solution)/shard_map/ppermute | solution.py:900
  997.5 74.0 %all-to-all-start.10 = ((bf16[8,1072,128]{2,1,0:T(8,128)(2,1)}), bf16[8,1072,128]{2,1,0:T(8,128)(2,1)}, u32[]{:S(2)}, u32[]{:S(2)}) async-start(bf16[8,1072,128]{2,1,0:T(8,128)(2,1)} %pad_maximum_fusion.1), calls=%async_computation.11 | async-start | bytes 4390912 | tf_op jit(solution)/shard_map/all_to_all | solution.py:924
  1020.2 1.9 collective-permute-start.19
  1022.7 22.8 %collective-permute-start.20 = (f32[2,1024]{1,0:T(2,128)S(1)}, f32[2,1024]{1,0:T(2,128)S(1)}, u32[]{:S(2)}, u32[]{:S(2)}) collective-permute-start(f32[2,1024]{1,0:T(2,128)S(1)} %fusion.112), channel_id=1, source_target_pairs={{0,2},{2,0},{1,3},{3,1},{4,6},{6,4},{5,7},{7,5},{8,10},{10,8},{9,1... | collective-permute-start | bytes 24584 | tf_op jit(solution)/shard_map/ppermute | solution.py:1098
  1046.2 8.1 copy-start.6
  1046.2 8.1 copy-start.59
  1046.3 6.5 collective-permute-start.21
  1050.6 19.1 %collective-permute-start.14 = (bf16[1,8,48,1024]{3,2,1,0:T(8,128)(2,1)S(1)}, bf16[1,8,48,1024]{3,2,1,0:T(8,128)(2,1)S(1)}, u32[]{:S(2)}, u32[]{:S(2)}) collective-permute-start(bf16[1,8,48,1024]{3,2,1,0:T(8,128)(2,1)S(1)} %dynamic-slice_bitcast_fusion.3), channel_id=1, source_target_pairs={{0,2},{2,0},{1,3},{3,1},{4,6},{6,4},{5,7},{7,5},{8,10},{10,8},{9,1... | collective-permute-start | bytes 2359304 | tf_op jit(solution)/shard_map/ppermute | solution.py:900
  1052.8 5.8 collective-permute-start.22
  1054.3 15.8 %copy-start.23 = (bf16[8,48,1024]{2,1,0:T(8,128)(2,1)S(1)}, bf16[8,48,1024]{2,1,0:T(8,128)(2,1)}, u32[]{:S(2)}) copy-start(bf16[8,48,1024]{2,1,0:T(8,128)(2,1)} %fusion.23) | copy-start | bytes 2359300
  1058.6 20.4 %collective-permute-start.23 = (f32[2,1024]{1,0:T(2,128)S(1)}, f32[2,1024]{1,0:T(2,128)S(1)}, u32[]{:S(2)}, u32[]{:S(2)}) collective-permute-start(f32[2,1024]{1,0:T(2,128)S(1)} %add.268), channel_id=1, source_target_pairs={{0,16},{4,20},{8,24},{12,28},{16,0},{20,4},{24,8},{28,12},{1,17},{... | collective-permute-start | bytes 24584 | tf_op jit(solution)/shard_map/ppermute | solution.py:1098
  1070.1 7.7 copy-start.17
  1071.4 7.5 copy-start.57
  1071.4 7.5 copy-start.62
  1071.4 7.5 copy-start.63
  1071.4 41.2 %all-to-all-start.9 = ((bf16[8,96,1024]{2,1,0:T(8,128)(2,1)}), bf16[8,96,1024]{2,1,0:T(8,128)(2,1)}, u32[]{:S(2)}, u32[]{:S(2)}) async-start(bf16[8,96,1024]{2,1,0:T(8,128)(2,1)} %pad_maximum_fusion.3), calls=%async_computation.10 | async-start | bytes 3145728 | tf_op jit(solution)/shard_map/all_to_all | solution.py:1043
  1077.8 8.9 copy-start.55
  1077.8 8.9 copy-start.56
  1078.8 12.6 %copy-start.34 = (f32[656,128]{1,0:T(8,128)S(1)}, f32[656,128]{1,0:T(8,128)}, u32[]{:S(2)}) copy-start(f32[656,128]{1,0:T(8,128)} %param.26) | copy-start | bytes 1007620
  1078.9 1.4 collective-permute-start.15
  1080.3 6.4 collective-permute-start.16
  1087.6 1.9 collective-permute-start.17
  1089.5 24.9 %copy-start.2 = (bf16[1,8,4,32,1024]{4,3,0,2,1:T(8,128)(2,1)S(1)}, bf16[1,8,4,32,1024]{4,3,0,2,1:T(8,128)(2,1)}, u32[]{:S(2)}) copy-start(bf16[1,8,4,32,1024]{4,3,0,2,1:T(8,128)(2,1)} %get-tuple-element.295) | copy-start | bytes 6291460
  1089.5 6.1 collective-permute-start.18
  1118.3 9.4 copy-start.29
  1118.3 30.9 %all-to-all-start.11 = ((bf16[8,544,128]{2,1,0:T(8,128)(2,1)}), bf16[8,544,128]{2,1,0:T(8,128)(2,1)S(1)}, u32[]{:S(2)}, u32[]{:S(2)}) async-start(bf16[8,544,128]{2,1,0:T(8,128)(2,1)} %pad_maximum_fusion.4), calls=%async_computation.12 | async-start | bytes 2228224 | tf_op jit(solution)/shard_map/all_to_all | solution.py:924
  1128.8 21.2 %copy-start.19 = (f32[128,768]{0,1:T(8,128)S(1)}, f32[128,768]{0,1:T(8,128)}, u32[]{:S(2)}) copy-start(f32[128,768]{0,1:T(8,128)} %copy-done.18) | copy-start | bytes 1179652
  1130.0 24.5 %copy-start.21 = (f32[128,768]{0,1:T(8,128)S(1)}, f32[128,768]{0,1:T(8,128)}, u32[]{:S(2)}) copy-start(f32[128,768]{0,1:T(8,128)} %copy-done.20) | copy-start | bytes 1179652
  (45 other events, 170.9 us)
Sparse Core Ops, SparseCore 0:
  11.5 61.7 all-gather.7
  76.7 96.6 all-gather.11
  176.9 193.5 all-gather.9
  373.8 121.4 all-gather.13
  518.9 230.2 reduce-scatter.1
where the time goes:
time: 1180 us; the launch traced here: 1170 us
  waiting for transfers between devices  391 us (33%)
  Pallas kernels  343 us (29%)
  starting transfers between devices  205 us (17%)
  local copies, waits for them, and re-layouts  102 us (9%)
  other arithmetic  73.1 us (6%)
  matrix products  38.2 us (3%)
  between operations  16.3 us (1%)
    pallas_call x2, Pallas kernels, attend_backward(): pl.pallas_call(backward_kernel, grid=(2, shards), in_specs=[pl.BlockSpec(...  161 us
    all_to_all x2, waiting for transfers between devices, body(): joints = [exchange(joint) for joint, _ in projected]  151 us
    ppermute x8, starting transfers between devices, halved(): other = lax.ppermute(other, axis, pairs)  98.1 us
    pallas_call x1, Pallas kernels, feed_forward(): pl.pallas_call(feed_kernel, grid=(GROUPS,), in_specs=[held, held, pl.Bloc...  81.5 us
    pallas_call x2, Pallas kernels, attend_forward(): pl.pallas_call(forward_kernel, grid=(2, half), in_specs=[pl.BlockSpec(mem...  64 us
    all_gather x4, waiting for transfers between devices, gathered(): flat = lax.all_gather(shard, everyone, axis=0, tiled=False)  60.6 us
    all_to_all x2, waiting for transfers between devices, body(): attends.append(exchange(attend.reshape(shards, HEAD_DIM, count)))  41.3 us
    all_to_all x2, waiting for transfers between devices, body(): grads.append(exchange(grad))  31.1 us
  transfers between devices with their start and end apart: 41, of which 22 were waited for; matrix products, arithmetic and copies ran while one was open for 15% of the time, Pallas kernels for 29%

commit v1 on v0

--- a/solution.py
+++ b/solution.py
@@ -80,54 +80,54 @@
     return jnp.where(place < limit, 0.0, MASK)
 
 
-def project_kernel(pieces_ref, first_ref, cosine_ref, sine_ref, out_ref, rows_ref):
-    shards, _, heads = pieces_ref.shape[:3]
-    lanes = pieces_ref.shape[-1]
-    weight = jnp.concatenate(
-        [pieces_ref[shard].reshape(3 * heads * HEAD_DIM, lanes) for shard in range(shards)], axis=1
-    )
-    product = lax.dot_general(weight, first_ref[...], NT, preferred_element_type=jnp.float32)
+def project_kernel(pieces_ref, first_ref, cosine_ref, sine_ref, out_ref, rows_ref, *, group):
+    shards, groups, size, _ = pieces_ref.shape
     cosine, sine = cosine_ref[...], sine_ref[...]
     half = HEAD_DIM // 2
-    for head in range(heads):
-        for part in range(3):
-            base = (part * heads + head) * HEAD_DIM
-            rows_ref[head, part] = weight[base : base + HEAD_DIM]
-        for part, scale in ((0, HEAD_DIM**-0.5), (1, 1.0)):
-            base = (part * heads + head) * HEAD_DIM
-            upper, lower = product[base : base + half], product[base + half : base + HEAD_DIM]
-            turned_upper = (upper * cosine - lower * sine).astype(jnp.bfloat16)
-            turned_lower = (lower * cosine + upper * sine).astype(jnp.bfloat16)
-            place = part * HEAD_DIM
-            out_ref[head, place : place + half, :] = turned_upper * jnp.bfloat16(scale)
-            out_ref[head, place + half : place + HEAD_DIM, :] = turned_lower * jnp.bfloat16(
-                scale
-            )
-        base = (2 * heads + head) * HEAD_DIM
-        out_ref[head, 2 * HEAD_DIM :, :] = product[base : base + HEAD_DIM].astype(jnp.bfloat16)
-
-
-def project_heads(pieces, first, cosine, sine):
-    shards, lanes = pieces.shape[0], pieces.shape[-1]
+
+    def chunk(part, head):
+        start = (part * shards + head) * HEAD_DIM
+        place = slice(start % size, start % size + HEAD_DIM)
+        return jnp.concatenate(
+            [pieces_ref[shard, start // size, place, :] for shard in range(shards)], axis=1
+        )
+
+    for begin in range(0, shards, group):
+        heads = range(begin, begin + group)
+        weight = jnp.concatenate([chunk(part, head) for head in heads for part in range(3)], axis=0)
+        product = lax.dot_general(weight, first_ref[...], NT, preferred_element_type=jnp.float32)
+        for index, head in enumerate(heads):
+            for part in range(3):
+                base = (3 * index + part) * HEAD_DIM
+                rows_ref[head, part] = weight[base : base + HEAD_DIM]
+            for part, scale in ((0, HEAD_DIM**-0.5), (1, 1.0)):
+                base = (3 * index + part) * HEAD_DIM
+                upper, lower = product[base : base + half], product[base + half : base + HEAD_DIM]
+                turned_upper = (upper * cosine - lower * sine).astype(jnp.bfloat16)
+                turned_lower = (lower * cosine + upper * sine).astype(jnp.bfloat16)
+                place = part * HEAD_DIM
+                scale = jnp.bfloat16(scale)
+                out_ref[head, place : place + half, :] = turned_upper * scale
+                out_ref[head, place + half : place + HEAD_DIM, :] = turned_lower * scale
+            base = (3 * index + 2) * HEAD_DIM
+            out_ref[head, 2 * HEAD_DIM :, :] = product[base : base + HEAD_DIM].astype(jnp.bfloat16)
+
+
+def project_heads(pieces, first, cosine, sine, phase):
+    shards, groups, _, size, lanes = pieces.shape
     count, width = first.shape
-    pieces = pieces.reshape(shards, 3, shards, HEAD_DIM, lanes)
-    group = min(4, shards)
     half = HEAD_DIM // 2
+    whole = lambda *shape: pl.BlockSpec(shape, lambda i: (0,) * len(shape))
     return pl.pallas_call(
-        project_kernel,
-        grid=(shards // group,),
+        functools.partial(project_kernel, group=min(4, shards)),
+        grid=(1,),
         in_specs=[
-            pl.BlockSpec(
-                (shards, 3, group, HEAD_DIM, lanes), lambda g: (0, 0, g, 0, 0)
-            ),
-            pl.BlockSpec((count, width), lambda g: (0, 0)),
-            pl.BlockSpec((half, count), lambda g: (0, 0)),
-            pl.BlockSpec((half, count), lambda g: (0, 0)),
+            pl.BlockSpec((shards, groups, None, size, lanes), lambda i: (0, 0, phase, 0, 0)),
+            whole(count, width),
+            whole(half, count),
+            whole(half, count),
         ],
-        out_specs=[
-            pl.BlockSpec((group, 3 * HEAD_DIM, count), lambda g: (g, 0, 0)),
-            pl.BlockSpec((group, 3, HEAD_DIM, width), lambda g: (g, 0, 0, 0)),
-        ],
+        out_specs=[whole(shards, 3 * HEAD_DIM, count), whole(shards, 3, HEAD_DIM, width)],
         out_shape=[
             jax.ShapeDtypeStruct((shards, 3 * HEAD_DIM, count), jnp.bfloat16),
             jax.ShapeDtypeStruct((shards, 3, HEAD_DIM, width), jnp.bfloat16),
@@ -750,10 +750,7 @@
         .transpose(1, 0, 2, 3)
         .reshape(phases, -1, piece)
     )
-    triple_pieces = [gathered(triple_shards[0])]
-    for phase in range(1, phases):
-        shard, triple_pieces[-1] = tied(triple_shards[phase], triple_pieces[-1])
-        triple_pieces.append(gathered(shard))
+    triple_pieces = gathered(triple_shards)
     output_columns = width // groups
     lanes = min(piece, output_columns)
 
@@ -768,11 +765,6 @@
     flat = tokens.reshape(count, width).astype(jnp.float32)
     first_normed, first_back = jax.vjp(layer_norm, flat, norm_gains[0])
     first_low = first_normed.astype(jnp.bfloat16)
-    projected = [
-        project_heads(pieces, first_low, cosine, sine) for pieces in triple_pieces
-    ]
-    triple_rows = [rows for _, rows in projected]
-    joints = [exchange(joint) for joint, _ in projected]
     other_shards = jnp.concatenate(
         [
             expand_weight.T.astype(jnp.bfloat16),
@@ -781,7 +773,12 @@
         ],
         axis=0,
     )
-    other_shards, joints[0] = tied(other_shards, joints[0])
+    other_shards, triple_pieces = tied(other_shards, triple_pieces)
+    projected = [
+        project_heads(triple_pieces, first_low, cosine, sine, phase) for phase in range(phases)
+    ]
+    triple_rows = [rows for _, rows in projected]
+    joints = [exchange(joint) for joint, _ in projected]
     other_pieces = gathered(other_shards)
     chosen = jnp.stack([bases_low[0], bases_low[2], bases_low[3]])
     chosen = lax.dynamic_slice_in_dim(chosen, member * base_rows, base_rows, 1)
@@ -805,6 +802,7 @@
             for start, end in ((0, expand_rows), (expand_rows, expand_rows + shrink_rows))
         ]
         feed_pieces = jnp.concatenate(feed_pieces, axis=2)
+    all_cosine, all_sine, joints[0] = tied(all_cosine, all_sine, joints[0])
     swap = functools.partial(lax.ppermute, axis_name="core", perm=[(0, 1), (1, 0)])
     both_lengths = jnp.concatenate([lengths, swap(lengths)])
     others, forwards, attends = [], [], []
@@ -869,7 +867,6 @@
     moments, bases_full, shrunk, second_change, parts = tied(
         moments, bases_full, shrunk, second_change, parts
     )
-    bases_full = bases_full.transpose(2, 0, 1, 3, 4).reshape(3, width, width)
     mixed, middle_back, branch_low, second_gain, *backs = leave_feed(
         output_rows,
         inside,
@@ -985,6 +982,8 @@
         step = back_product(direction.astype(jnp.bfloat16), base)
         return rotated.astype(jnp.bfloat16), step.astype(jnp.bfloat16)
 
+    output_terms = widened(output_terms)
+    output_terms, attend_backs[0] = tied(output_terms, attend_backs[0])
     other_backs, grads = [], []
     for phase in range(phases):
         other_backs.append(swap(attend_backs[phase]))
@@ -999,15 +998,17 @@
             all_sine,
         )
         if phase < phases - 1:
-            attend_backs[phase + 1], output_terms, own_grad, other_grad = tied(
-                attend_backs[phase + 1], output_terms, own_grad, other_grad
+            attend_backs[phase + 1], own_grad, other_grad = tied(
+                attend_backs[phase + 1], own_grad, other_grad
             )
         else:
-            grads, owned, own_grad, other_grad = tied(grads, owned, own_grad, other_grad)
+            grads, owned, bases_full, own_grad, other_grad = tied(
+                grads, owned, bases_full, own_grad, other_grad
+            )
         grad = own_grad.astype(jnp.float32) + swap(other_grad).astype(jnp.float32)
         grad = grad.astype(jnp.bfloat16)
         if phase == 0:
-            grad = jnp.concatenate([grad, widened(output_terms)], axis=1)
+            grad = jnp.concatenate([grad, output_terms], axis=1)
         grads.append(exchange(grad))
     output_low = halved(far_sum(narrowed(grads[0][:, 3 * HEAD_DIM :])), "outer", 0)
     grads[0] = grads[0][:, : 3 * HEAD_DIM]
@@ -1024,6 +1025,7 @@
         rows = far_sum(terms)
         return jnp.concatenate([rows, *soap_rows(rows, bases_full[0], moments[2 + phase])])
 
+    bases_full = bases_full.transpose(2, 0, 1, 3, 4).reshape(3, width, width)
     last = phases - 1
     summed = [triple_sum(grads[phase]) for phase in range(last)]
     feed_rows = jnp.concatenate(
@@ -1033,10 +1035,12 @@
             *soap_rows(owned[expand_height:], bases_full[2], moments[1]),
         ]
     )
-    grads[last], summed, feed_rows, output_left = tied(
-        grads[last], summed, feed_rows, output_left
-    )
-    settled, output_left = merged(cut_rows(feed_rows), output_left)
+    settled = jnp.concatenate(
+        [cut_rows(feed_rows), output_left.reshape(shards, -1, piece)], axis=1
+    )
+    grads[last], summed, settled = tied(grads[last], summed, settled)
+    settled = exchange(settled)
+    output_left = settled[:, feed_rows.shape[0] :].reshape(shards, piece, output_columns)
     output_left = far_sum(output_left)
     summed.append(triple_sum(grads[last]))
     joint_backs = [joint_back for _, joint_back in summed]

time: 1180 us -> 1260 us (1.068)
  starting transfers between devices: 205 us -> 260 us
  Pallas kernels: 343 us -> 396 us
  waiting for transfers between devices: 391 us -> 349 us
    pallas_call x2, Pallas kernels: 161 us -> 206 us  [attend_backward(): pl.pallas_call(backward_kernel, grid=(2, shards), in_specs=[pl.BlockSpec(...]
    ppermute x8, starting transfers between devices: 98.1 us -> 130 us  [halved(): other = lax.ppermute(other, axis, pairs)]
    all_to_all x2, starting transfers between devices: 24 us -> 49.3 us  [body(): grads.append(exchange(grad))]
    all_to_all x2, waiting for transfers between devices: 31.1 us -> 7.73 us  [body(): grads.append(exchange(grad))]
    all_to_all x2, waiting for transfers between devices: 41.3 us -> 21.1 us  [body(): attends.append(exchange(attend.reshape(shards, HEAD_DIM, count)))]
    pallas_call x2, Pallas kernels: 64 us -> 81.5 us  [attend_forward(): pl.pallas_call(forward_kernel, grid=(2, half), in_specs=[pl.BlockSpec(mem...]
    all_to_all x2, waiting for transfers between devices: 28.3 us -> 12 us  [body(): attend_backs = [exchange(back) for back in backs]]
    all_gather x4 -> x3, waiting for transfers between devices: 60.6 us -> 71.6 us  [gathered(): flat = lax.all_gather(shard, everyone, axis=0, tiled=False)]
  transfers between devices with their start and end apart: 41 -> 40, of which waited for: 22 -> 23; matrix products, arithmetic and copies ran while one was open for 15% -> 14% of each run, Pallas kernels for 29% -> 32%
where the time goes in v1:
time: 1260 us; the launch traced here: 1240 us
  Pallas kernels  396 us (31%)
  waiting for transfers between devices  349 us (28%)
  starting transfers between devices  260 us (21%)
  local copies, waits for them, and re-layouts  105 us (8%)
  other arithmetic  72.5 us (6%)
  matrix products  39.1 us (3%)
  between operations  16.3 us (1%)
    pallas_call x2, Pallas kernels, attend_backward(): pl.pallas_call(backward_kernel, grid=(2, shards), in_specs=[pl.BlockSpec(...  206 us
    all_to_all x2, waiting for transfers between devices, body(): joints = [exchange(joint) for joint, _ in projected]  155 us
    ppermute x8, starting transfers between devices, halved(): other = lax.ppermute(other, axis, pairs)  130 us
    pallas_call x2, Pallas kernels, attend_forward(): pl.pallas_call(forward_kernel, grid=(2, half), in_specs=[pl.BlockSpec(mem...  81.5 us
    all_gather x3, waiting for transfers between devices, gathered(): flat = lax.all_gather(shard, everyone, axis=0, tiled=False)  71.6 us
    pallas_call x1, Pallas kernels, feed_forward(): pl.pallas_call(feed_kernel, grid=(GROUPS,), in_specs=[held, held, pl.Bloc...  70.9 us
    all_to_all x2, starting transfers between devices, body(): grads.append(exchange(grad))  49.3 us
    unnamed x169, local copies, waits for them, and re-layouts  32.4 us
  transfers between devices with their start and end apart: 40, of which 23 were waited for; matrix products, arithmetic and copies ran while one was open for 14% of the time, Pallas kernels for 32%

profile of v1, /device:TPU:0, one launch (start us, length us, event | category | flops | bytes accessed | tf_op | source)
XLA Modules:
  0.0 1237.8 jit_solution(9101563214210171888)
XLA Ops:
  12.3 71.6 %all-gather.6.cloned.1.call-done = bf16[32,2,384,128]{3,2,1,0:T(8,128)(2,1)} async-done(((bf16[1,2,384,128]{3,2,1,0:T(8,128)(2,1)}), bf16[32,2,384,128]{3,2,1,0:T(8,128)(2,1)}) %all-gather.6.cloned.1.call-update) | async-done | bytes 6291472 | tf_op jit(solution)/shard_map/all_gather | solution.py:744
  88.3 7.9 shard_map.396
  96.1 4.0 all-to-all-start.1
  100.1 7.7 shard_map.395
  107.8 94.9 %all-to-all-done.1.own_ref = bf16[8,192,1024]{2,1,0:T(8,128)(2,1)S(1)} async-done(((bf16[8,192,1024]{2,1,0:T(8,128)(2,1)}), bf16[8,192,1024]{2,1,0:T(8,128)(2,1)S(1)}, u32[]{:S(2)}, u32[]{:S(2)}) %all-to-all-start.1) | async-done | bytes 3145760 | tf_op jit(solution)/shard_map/all_to_all | solution.py:781
  204.8 3.9 all-to-all-start
  208.7 4.8 multiply_sine_fusion
  214.7 5.0 collective-permute-done
  220.9 40.7 %shard_map.397 = (bf16[2,4,64,1024]{3,2,1,0:T(8,128)(2,1)}, f32[2,4,1,1024]{3,2,1,0:T(1,128)}) custom-call(s32[2]{0:T(128)} %pad_add_fusion.length_ref, bf16[8,192,1024]{2,1,0:T(8,128)(2,1)} %copy-done.4, bf16[8,192,1024]{2,1,0:T(8,128)(2,1)} %collective-permute-done.1.other_ref), custom_call_target="tpu_custom_call" | custom-call | flops 67108864 | bytes 524288 | tf_op jit(solution)/shard_map/pallas_call | solution.py:243
  261.6 59.9 %all-to-all-done.own_ref = bf16[8,192,1024]{2,1,0:T(8,128)(2,1)S(1)} async-done(((bf16[8,192,1024]{2,1,0:T(8,128)(2,1)}), bf16[8,192,1024]{2,1,0:T(8,128)(2,1)S(1)}, u32[]{:S(2)}, u32[]{:S(2)}) %all-to-all-start) | async-done | bytes 3145760 | tf_op jit(solution)/shard_map/all_to_all | solution.py:781
  323.8 4.1 collective-permute-done.2
  329.2 4.2 all-to-all-start.2
  338.4 40.7 %shard_map.398 = (bf16[2,4,64,1024]{3,2,1,0:T(8,128)(2,1)}, f32[2,4,1,1024]{3,2,1,0:T(1,128)}) custom-call(s32[2]{0:T(128)} %pad_add_fusion.length_ref, bf16[8,192,1024]{2,1,0:T(8,128)(2,1)} %copy-done.3, bf16[8,192,1024]{2,1,0:T(8,128)(2,1)} %collective-permute-done.3.other_ref), custom_call_target="tpu_custom_call" | custom-call | flops 67108864 | bytes 524288 | tf_op jit(solution)/shard_map/pallas_call | solution.py:243
  380.5 3.3 collective-permute-start.4
  386.6 5.6 all-to-all-start.3
  398.8 21.1 %all-to-all-done.3 = bf16[8,64,1024]{2,1,0:T(8,128)(2,1)S(1)} async-done(((bf16[8,64,1024]{2,1,0:T(8,128)(2,1)}), bf16[8,64,1024]{2,1,0:T(8,128)(2,1)S(1)}, u32[]{:S(2)}, u32[]{:S(2)}) %all-to-all-start.3) | async-done | bytes 1048608 | tf_op jit(solution)/shard_map/all_to_all | solution.py:818
  429.1 3.6 all-to-all-start.4
  436.7 2.5 fusion.125
  439.2 2.6 unstack.37.refs_2_.refs_0_
  441.8 2.6 unstack.39.refs_3_.refs_1_
  444.3 9.4 shard_map.399
  453.8 70.9 %shard_map.400 = (f32[1024,1024]{1,0:T(8,128)}, f32[1024,1024]{1,0:T(8,128)}, bf16[8,4,272,1024]{3,2,1,0:T(8,128)(2,1)}) custom-call(bf16[1024,1024]{1,0:T(8,128)(2,1)} %get-tuple-element.126.second_ref, bf16[1024,1024]{1,0:T(8,128)(2,1)} %get-tuple-element.127.upstream_ref.refs_8_, bf16[8,4,2224,128]{3,2,1,0:T(8,128)(2,1)} %bitcast.325, ...), custom_call_target="tpu_custom_call" | custom-call | flops 1048576 | bytes 1048576 | tf_op jit(solution)/shard_map/pallas_call | solution.py:557
  530.2 12.6 %shard_map.401 = (bf16[1024,1024]{1,0:T(8,128)(2,1)}, f32[1024,1024]{1,0:T(8,128)}, bf16[1024,1024]{1,0:T(8,128)(2,1)}, f32[1,1024]{1,0:T(1,128)}, bf16[512,1024]{1,0:T(8,128)(2,1)}, /*index=5*/bf16[512,1024]{1,0:T(8,128)(2,1)}) custom-call(bf16[512,1024]{1,0:T(8,128)(2,1)} %unstack.37.refs_2_.refs_0_, bf16[512,1024]{1,0:T(8,128)(2,1)} %unstack.39.refs_3_.refs_1_, ...), custom_call_target="tpu_custom_call" | custom-call | flops 2147483648 | bytes 29360128 | tf_op jit(solution)/shard_map/pallas_call | solution.py:672
  542.8 4.6 all-to-all-start.6
  547.4 3.3 convolution_convert_fusion.3
  553.5 3.3 reshape.473
  556.8 5.6 constant_dynamic-slice_fusion.3
  563.7 12.0 all-to-all-done.6.own_back_ref
  576.6 3.6 all-to-all-start.5
  584.2 2.8 collective-permute-done.6.other_back_ref
  588.0 102.9 %shard_map.402 = (bf16[8,192,1024]{2,1,0:T(8,128)(2,1)}, bf16[8,192,1024]{2,1,0:T(8,128)(2,1)}) custom-call(s32[2]{0:T(128)} %pad_add_fusion.length_ref, bf16[8,192,1024]{2,1,0:T(8,128)(2,1)} %copy-done.4, bf16[8,192,1024]{2,1,0:T(8,128)(2,1)} %collective-permute-done.1.other_ref, bf16[8,64,1024]{2,1,0:T(8,128)(2,1)} %copy-done.20, ...), custom_call_target="tpu_custom_call" | custom-call | flops 67108864 | bytes 524288 | tf_op jit(solution)/shard_map/pallas_call | solution.py:391
  690.9 7.6 collective-permute-start.7
  698.5 5.5 collective-permute-done.7
  704.0 3.5 add_convert_fusion.1
  707.5 2.8 pad_maximum_fusion
  710.4 5.9 all-to-all-start.7
  716.4 2.6 collective-permute-done.8.other_back_ref
  720.0 103.3 %shard_map.403 = (bf16[8,192,1024]{2,1,0:T(8,128)(2,1)}, bf16[8,192,1024]{2,1,0:T(8,128)(2,1)}) custom-call(s32[2]{0:T(128)} %pad_add_fusion.length_ref, bf16[8,192,1024]{2,1,0:T(8,128)(2,1)} %copy-done.3, bf16[8,192,1024]{2,1,0:T(8,128)(2,1)} %collective-permute-done.3.other_ref, bf16[8,64,1024]{2,1,0:T(8,128)(2,1)} %copy-done.19, ...), custom_call_target="tpu_custom_call" | custom-call | flops 67108864 | bytes 524288 | tf_op jit(solution)/shard_map/pallas_call | solution.py:391
  823.3 7.7 all-to-all-done.7
  831.1 5.9 collective-permute-done.9
  836.9 5.2 add_convert_fusion
  842.1 43.4 %all-to-all-start.8 = ((bf16[8,192,1024]{2,1,0:T(8,128)(2,1)}), bf16[8,192,1024]{2,1,0:T(8,128)(2,1)}, u32[]{:S(2)}, u32[]{:S(2)}) async-start(bf16[8,192,1024]{2,1,0:T(8,128)(2,1)} %add_convert_fusion), calls=%async_computation.9 | async-start | bytes 6291456 | tf_op jit(solution)/shard_map/all_to_all | solution.py:1012
  885.5 2.3 slice.183
  888.1 3.9 convolution_convert_fusion.1
  895.4 3.1 fusion.122
  904.7 123.6 %collective-permute-start.12 = (bf16[1,128,256]{2,1,0:T(8,128)(2,1)S(1)}, bf16[1,128,256]{2,1,0:T(8,128)(2,1)S(1)}, u32[]{:S(2)}, u32[]{:S(2)}) collective-permute-start(bf16[1,128,256]{2,1,0:T(8,128)(2,1)S(1)} %constant_dynamic-slice_fusion.2), channel_id=1, source_target_pairs={{0,2},{2,0},{1,3},{3,1},{4,6},{6,4},{5,7},{7,5},{8,10},{10,8},{9,1... | collective-permute-start | bytes 196616 | tf_op jit(solution)/shard_map/ppermute | solution.py:897
  1047.4 3.2 pad_maximum_fusion.1
  1050.6 9.4 collective-permute-done.11
  1060.0 2.3 fusion.22
  1062.3 5.8 convolution_convert_fusion
  1071.5 6.3 all-to-all-start.10
  1077.8 6.5 fusion.132
  1084.3 6.2 fusion.9
  1090.5 3.0 fusion.7
  1096.8 16.6 %collective-permute-start.20 = (f32[2,1024]{1,0:T(2,128)S(1)}, f32[2,1024]{1,0:T(2,128)S(1)}, u32[]{:S(2)}, u32[]{:S(2)}) collective-permute-start(f32[2,1024]{1,0:T(2,128)S(1)} %fusion.111), channel_id=1, source_target_pairs={{0,2},{2,0},{1,3},{3,1},{4,6},{6,4},{5,7},{7,5},{8,10},{10,8},{9,1... | collective-permute-start | bytes 24584 | tf_op jit(solution)/shard_map/ppermute | solution.py:1102
  1117.5 2.6 fusion.10
  1124.0 4.3 fusion.13
  1130.6 8.7 collective-permute-done.14
  1141.0 5.2 all-to-all-start.9
  1149.9 4.0 collective-permute-start.16
  1161.8 3.3 collective-permute-done.18
  1171.4 10.8 all-to-all-done.9
  1187.8 3.7 all-to-all-start.11
  1199.5 19.1 %all-to-all-done.11 = bf16[8,544,128]{2,1,0:T(8,128)(2,1)S(1)} async-done(((bf16[8,544,128]{2,1,0:T(8,128)(2,1)}), bf16[8,544,128]{2,1,0:T(8,128)(2,1)S(1)}, u32[]{:S(2)}, u32[]{:S(2)}) %all-to-all-start.11) | async-done | bytes 1114144 | tf_op jit(solution)/shard_map/all_to_all | solution.py:921
  (341 shorter events, 152.3 us)
Async XLA Ops:
  7.2 76.7 %copy-start.61 = (f32[2,1024]{1,0:T(2,128)S(1)}, f32[2,1024]{1,0:T(2,128)}, u32[]{:S(2)}) copy-start(f32[2,1024]{1,0:T(2,128)} %refs_9_.1) | copy-start | bytes 24580
  7.2 76.7 %copy-start = (bf16[1,1024,1024]{2,1,0:T(8,128)(2,1)S(1)}, bf16[1,1024,1024]{2,1,0:T(8,128)(2,1)}, u32[]{:S(2)}) copy-start(bf16[1,1024,1024]{2,1,0:T(8,128)(2,1)} %param.20) | copy-start | bytes 6291460
  7.2 76.6 %all-gather.6.cloned.1.call-start = ((), (), s32[]{:S(2)}) async-start(), calls=%async_computation.13 | async-start | bytes 6488064 | tf_op jit(solution)/shard_map/all_gather | solution.py:744
  8.6 75.7 %copy-start.24 = (f32[128,768]{0,1:T(8,128)}, f32[128,768]{0,1:T(8,128)S(1)}, u32[]{:S(2)}) copy-start(f32[128,768]{0,1:T(8,128)S(1)} %copy.207) | copy-start | bytes 1179652
  9.4 410.5 %all-gather.8.cloned.1.call-start = ((), (), s32[]{:S(2)}) async-start(), calls=%async_computation.15 | async-start | bytes 18788352 | tf_op jit(solution)/shard_map/all_gather | solution.py:744
  96.1 106.7 %all-to-all-start.1 = ((bf16[8,192,1024]{2,1,0:T(8,128)(2,1)}), bf16[8,192,1024]{2,1,0:T(8,128)(2,1)S(1)}, u32[]{:S(2)}, u32[]{:S(2)}) async-start(bf16[8,192,1024]{2,1,0:T(8,128)(2,1)} %get-tuple-element.105), calls=%async_computation.1 | async-start | bytes 6291456 | tf_op jit(solution)/shard_map/all_to_all | solution.py:781
  204.8 116.7 %all-to-all-start = ((bf16[8,192,1024]{2,1,0:T(8,128)(2,1)}), bf16[8,192,1024]{2,1,0:T(8,128)(2,1)S(1)}, u32[]{:S(2)}, u32[]{:S(2)}) async-start(bf16[8,192,1024]{2,1,0:T(8,128)(2,1)} %get-tuple-element.104), calls=%async_computation | async-start | bytes 6291456 | tf_op jit(solution)/shard_map/all_to_all | solution.py:781
  213.6 7.3 collective-permute-start.1
  213.6 6.1 collective-permute-start
  321.6 16.9 %collective-permute-start.3 = (bf16[8,192,1024]{2,1,0:T(8,128)(2,1)S(1)}, bf16[8,192,1024]{2,1,0:T(8,128)(2,1)}, u32[]{:S(2)}, u32[]{:S(2)}) collective-permute-start(bf16[8,192,1024]{2,1,0:T(8,128)(2,1)S(1)} %all-to-all-done.own_ref), channel_id=1, source_target_pairs={{0,1},{1,0},{2,3},{3,2},{4,5},{5,4},{6,7},{7,6},{8,9},{9,8},{10,11... | collective-permute-start | bytes 9437192 | tf_op jit(solution)/shard_map/ppermute | solution.py:810
  323.6 4.3 collective-permute-start.2
  329.2 50.0 %all-to-all-start.2 = ((bf16[8,64,1024]{2,1,0:T(8,128)(2,1)}), bf16[8,64,1024]{2,1,0:T(8,128)(2,1)}, u32[]{:S(2)}, u32[]{:S(2)}) async-start(bf16[8,64,1024]{2,1,0:T(8,128)(2,1)} %bitcast.352), calls=%async_computation.2 | async-start | bytes 2097152 | tf_op jit(solution)/shard_map/all_to_all | solution.py:818
  333.4 196.8 %all-gather.10.cloned.1.call-start = ((), (), s32[]{:S(2)}) async-start(), calls=%async_computation.16 | async-start | bytes 6488064 | tf_op jit(solution)/shard_map/all_gather | solution.py:744
  380.5 4.9 collective-permute-start.4
  386.6 33.3 %all-to-all-start.3 = ((bf16[8,64,1024]{2,1,0:T(8,128)(2,1)}), bf16[8,64,1024]{2,1,0:T(8,128)(2,1)S(1)}, u32[]{:S(2)}, u32[]{:S(2)}) async-start(bf16[8,64,1024]{2,1,0:T(8,128)(2,1)} %bitcast.41), calls=%async_computation.3 | async-start | bytes 2097152 | tf_op jit(solution)/shard_map/all_to_all | solution.py:818
  392.5 28.4 %copy-start.26 = (f32[128,768]{0,1:T(8,128)}, f32[128,768]{0,1:T(8,128)S(1)}, u32[]{:S(2)}) copy-start(f32[128,768]{0,1:T(8,128)S(1)} %copy.211) | copy-start | bytes 1179652
  419.9 9.2 copy-start.17
  419.9 7.7 copy-start.42
  429.1 97.0 %all-to-all-start.4 = ((f32[8,736,128]{2,1,0:T(8,128)}), f32[8,736,128]{2,1,0:T(8,128)S(1)}, u32[]{:S(2)}, u32[]{:S(2)}) async-start(f32[8,736,128]{2,1,0:T(8,128)} %constant_dynamic-update-slice_fusion), calls=%async_computation.4 | async-start | bytes 6029312 | tf_op jit(solution)/shard_map/all_to_all | solution.py:826
  432.8 398.3 %reduce-scatter.2.cloned.1.call-start = ((), (), s32[]{:S(2)}) async-start(), calls=%async_computation.14 | async-start | bytes 18382848 | tf_op jit(solution)/shard_map/reduce_scatter | solution.py:976
  542.8 32.9 %all-to-all-start.6 = ((bf16[8,64,1024]{2,1,0:T(8,128)(2,1)}), bf16[8,64,1024]{2,1,0:T(8,128)(2,1)S(1)}, u32[]{:S(2)}, u32[]{:S(2)}) async-start(bf16[8,64,1024]{2,1,0:T(8,128)(2,1)} %bitcast.376), calls=%async_computation.6 | async-start | bytes 2097152 | tf_op jit(solution)/shard_map/all_to_all | solution.py:884
  562.5 17.7 %copy-start.10 = (bf16[8,128,2,1,256]{4,3,2,1,0:T(2,128)(2,1)S(1)}, bf16[8,128,2,1,256]{4,3,2,1,0:T(2,128)(2,1)}, u32[]{:S(2)}) copy-start(bf16[8,128,2,1,256]{4,3,2,1,0:T(2,128)(2,1)} %get-tuple-element.342) | copy-start | bytes 3145732
  563.7 16.5 %collective-permute-start.5 = (bf16[8,2,1,128,256]{4,3,2,1,0:T(8,128)(2,1)}, bf16[8,2,1,128,256]{4,3,2,1,0:T(8,128)(2,1)}, u32[]{:S(2)}, u32[]{:S(2)}) collective-permute-start(bf16[8,2,1,128,256]{4,3,2,1,0:T(8,128)(2,1)} %copy.225), channel_id=1, source_target_pairs={{0,1},{1,0},{2,3},{3,2},{4,5},{5,4},{6,7},{7,6},{8,9},{9,8},{10,11... | collective-permute-start | bytes 3145736 | tf_op jit(solution)/shard_map/ppermute | solution.py:897
  576.6 114.2 %all-to-all-start.5 = ((bf16[8,64,1024]{2,1,0:T(8,128)(2,1)}), bf16[8,64,1024]{2,1,0:T(8,128)(2,1)S(1)}, u32[]{:S(2)}, u32[]{:S(2)}) async-start(bf16[8,64,1024]{2,1,0:T(8,128)(2,1)} %bitcast.375), calls=%async_computation.5 | async-start | bytes 2097152 | tf_op jit(solution)/shard_map/all_to_all | solution.py:884
  584.2 2.8 collective-permute-start.6
  690.9 25.4 %copy-start.19 = (bf16[8,64,1024]{2,1,0:T(8,128)(2,1)}, bf16[8,64,1024]{2,1,0:T(8,128)(2,1)S(1)}, u32[]{:S(2)}) copy-start(bf16[8,64,1024]{2,1,0:T(8,128)(2,1)S(1)} %all-to-all-done.5.own_back_ref) | copy-start | bytes 3145732
  690.9 16.7 %copy-start.23 = (bf16[8,64,1024]{2,1,0:T(8,128)(2,1)S(1)}, bf16[8,64,1024]{2,1,0:T(8,128)(2,1)}, u32[]{:S(2)}) copy-start(bf16[8,64,1024]{2,1,0:T(8,128)(2,1)} %reshape.474) | copy-start | bytes 3145732
  690.9 13.1 %collective-permute-start.7 = (bf16[8,192,1024]{2,1,0:T(8,128)(2,1)}, bf16[8,192,1024]{2,1,0:T(8,128)(2,1)S(1)}, u32[]{:S(2)}, u32[]{:S(2)}) collective-permute-start(bf16[8,192,1024]{2,1,0:T(8,128)(2,1)} %get-tuple-element.149), channel_id=1, source_target_pairs={{0,1},{1,0},{2,3},{3,2},{4,5},{5,4},{6,7},{7,6},{8,9},{9,8},{10,11... | collective-permute-start | bytes 9437192 | tf_op jit(solution)/shard_map/ppermute | solution.py:1008
  710.4 120.7 %all-to-all-start.7 = ((bf16[8,256,1024]{2,1,0:T(8,128)(2,1)}), bf16[8,256,1024]{2,1,0:T(8,128)(2,1)}, u32[]{:S(2)}, u32[]{:S(2)}) async-start(bf16[8,256,1024]{2,1,0:T(8,128)(2,1)} %pad_maximum_fusion), calls=%async_computation.7 | async-start | bytes 8388608 | tf_op jit(solution)/shard_map/all_to_all | solution.py:1012
  716.3 2.7 collective-permute-start.8
  831.1 5.9 collective-permute-start.9
  842.1 220.2 %all-to-all-start.8 = ((bf16[8,192,1024]{2,1,0:T(8,128)(2,1)}), bf16[8,192,1024]{2,1,0:T(8,128)(2,1)}, u32[]{:S(2)}, u32[]{:S(2)}) async-start(bf16[8,192,1024]{2,1,0:T(8,128)(2,1)} %add_convert_fusion), calls=%async_computation.9 | async-start | bytes 6291456 | tf_op jit(solution)/shard_map/all_to_all | solution.py:1012
  895.4 140.4 %collective-permute-start.10 = (bf16[2,1,8,48,1024]{4,3,2,0,1:T(8,128)(2,1)}, bf16[2,1,8,48,1024]{4,3,2,0,1:T(8,128)(2,1)}, u32[]{:S(2)}, u32[]{:S(2)}) collective-permute-start(bf16[2,1,8,48,1024]{4,3,2,0,1:T(8,128)(2,1)} %dynamic-slice_bitcast_fusion.2), channel_id=1, source_target_pairs={{0,1},{1,0},{2,3},{3,2},{4,5},{5,4},{6,7},{7,6},{8,9},{9,8},{10,11... | collective-permute-start | bytes 4718600 | tf_op jit(solution)/shard_map/ppermute | solution.py:897
  903.7 128.0 %copy-start.11 = (bf16[1,8,4,32,1024]{4,3,0,2,1:T(8,128)(2,1)S(1)}, bf16[1,8,4,32,1024]{4,3,0,2,1:T(8,128)(2,1)}, u32[]{:S(2)}) copy-start(bf16[1,8,4,32,1024]{4,3,0,2,1:T(8,128)(2,1)} %get-tuple-element.327) | copy-start | bytes 6291460
  903.7 128.0 %copy-start.47 = (f32[176,1024]{1,0:T(8,128)S(1)}, f32[176,1024]{1,0:T(8,128)}, u32[]{:S(2)}) copy-start(f32[176,1024]{1,0:T(8,128)} %get-tuple-element.164) | copy-start | bytes 2162692
  903.7 128.0 %copy-start.48 = (f32[176,1024]{1,0:T(8,128)S(1)}, f32[176,1024]{1,0:T(8,128)}, u32[]{:S(2)}) copy-start(f32[176,1024]{1,0:T(8,128)} %get-tuple-element.163) | copy-start | bytes 2162692
  904.7 136.9 %collective-permute-start.12 = (bf16[1,128,256]{2,1,0:T(8,128)(2,1)S(1)}, bf16[1,128,256]{2,1,0:T(8,128)(2,1)S(1)}, u32[]{:S(2)}, u32[]{:S(2)}) collective-permute-start(bf16[1,128,256]{2,1,0:T(8,128)(2,1)S(1)} %constant_dynamic-slice_fusion.2), channel_id=1, source_target_pairs={{0,2},{2,0},{1,3},{3,1},{4,6},{6,4},{5,7},{7,5},{8,10},{10,8},{9,1... | collective-permute-start | bytes 196616 | tf_op jit(solution)/shard_map/ppermute | solution.py:897
  1040.0 20.0 %collective-permute-start.11 = (bf16[1,8,48,1024]{3,2,1,0:T(8,128)(2,1)}, bf16[1,8,48,1024]{3,2,1,0:T(8,128)(2,1)}, u32[]{:S(2)}, u32[]{:S(2)}) collective-permute-start(bf16[1,8,48,1024]{3,2,1,0:T(8,128)(2,1)} %dynamic-slice_bitcast_fusion.4), channel_id=1, source_target_pairs={{0,2},{2,0},{1,3},{3,1},{4,6},{6,4},{5,7},{7,5},{8,10},{10,8},{9,1... | collective-permute-start | bytes 2359304 | tf_op jit(solution)/shard_map/ppermute | solution.py:897
  1047.4 12.6 %copy-start.14 = (bf16[2,1,8,48,1024]{4,3,2,0,1:T(8,128)(2,1)S(1)}, bf16[2,1,8,48,1024]{4,3,2,0,1:T(8,128)(2,1)}, u32[]{:S(2)}) copy-start(bf16[2,1,8,48,1024]{4,3,2,0,1:T(8,128)(2,1)} %copy-done.13) | copy-start | bytes 4718596
  1071.5 46.0 %collective-permute-start.13 = (bf16[2,1,8,48,1024]{4,3,2,1,0:T(8,128)(2,1)}, bf16[2,1,8,48,1024]{4,3,2,1,0:T(8,128)(2,1)}, u32[]{:S(2)}, u32[]{:S(2)}) collective-permute-start(bf16[2,1,8,48,1024]{4,3,2,1,0:T(8,128)(2,1)} %dynamic-slice_bitcast_fusion.1), channel_id=1, source_target_pairs={{0,1},{1,0},{2,3},{3,2},{4,5},{5,4},{6,7},{7,6},{8,9},{9,8},{10,11... | collective-permute-start | bytes 4718600 | tf_op jit(solution)/shard_map/ppermute | solution.py:897
  1071.5 69.5 %all-to-all-start.10 = ((bf16[8,1072,128]{2,1,0:T(8,128)(2,1)}), bf16[8,1072,128]{2,1,0:T(8,128)(2,1)}, u32[]{:S(2)}, u32[]{:S(2)}) async-start(bf16[8,1072,128]{2,1,0:T(8,128)(2,1)} %pad_maximum_fusion.1), calls=%async_computation.11 | async-start | bytes 4390912 | tf_op jit(solution)/shard_map/all_to_all | solution.py:1042
  1094.2 1.9 collective-permute-start.19
  1096.8 18.2 %collective-permute-start.20 = (f32[2,1024]{1,0:T(2,128)S(1)}, f32[2,1024]{1,0:T(2,128)S(1)}, u32[]{:S(2)}, u32[]{:S(2)}) collective-permute-start(f32[2,1024]{1,0:T(2,128)S(1)} %fusion.111), channel_id=1, source_target_pairs={{0,2},{2,0},{1,3},{3,1},{4,6},{6,4},{5,7},{7,5},{8,10},{10,8},{9,1... | collective-permute-start | bytes 24584 | tf_op jit(solution)/shard_map/ppermute | solution.py:1102
  1115.8 8.2 copy-start.6
  1115.8 8.2 copy-start.64
  1115.8 6.5 collective-permute-start.21
  1120.2 19.1 %collective-permute-start.14 = (bf16[1,8,48,1024]{3,2,1,0:T(8,128)(2,1)S(1)}, bf16[1,8,48,1024]{3,2,1,0:T(8,128)(2,1)S(1)}, u32[]{:S(2)}, u32[]{:S(2)}) collective-permute-start(bf16[1,8,48,1024]{3,2,1,0:T(8,128)(2,1)S(1)} %dynamic-slice_bitcast_fusion.3), channel_id=1, source_target_pairs={{0,2},{2,0},{1,3},{3,1},{4,6},{6,4},{5,7},{7,5},{8,10},{10,8},{9,1... | collective-permute-start | bytes 2359304 | tf_op jit(solution)/shard_map/ppermute | solution.py:897
  1122.3 6.7 collective-permute-start.22
  1124.0 15.7 %copy-start.29 = (bf16[8,48,1024]{2,1,0:T(8,128)(2,1)S(1)}, bf16[8,48,1024]{2,1,0:T(8,128)(2,1)}, u32[]{:S(2)}) copy-start(bf16[8,48,1024]{2,1,0:T(8,128)(2,1)} %fusion.22) | copy-start | bytes 2359300
  1129.0 19.5 %collective-permute-start.23 = (f32[2,1024]{1,0:T(2,128)S(1)}, f32[2,1024]{1,0:T(2,128)S(1)}, u32[]{:S(2)}, u32[]{:S(2)}) collective-permute-start(f32[2,1024]{1,0:T(2,128)S(1)} %add.268), channel_id=1, source_target_pairs={{0,16},{4,20},{8,24},{12,28},{16,0},{20,4},{24,8},{28,12},{1,17},{... | collective-permute-start | bytes 24584 | tf_op jit(solution)/shard_map/ppermute | solution.py:1102
  1139.7 7.7 copy-start.22
  1141.0 41.2 %all-to-all-start.9 = ((bf16[8,96,1024]{2,1,0:T(8,128)(2,1)}), bf16[8,96,1024]{2,1,0:T(8,128)(2,1)}, u32[]{:S(2)}, u32[]{:S(2)}) async-start(bf16[8,96,1024]{2,1,0:T(8,128)(2,1)} %pad_maximum_fusion.3), calls=%async_computation.10 | async-start | bytes 3145728 | tf_op jit(solution)/shard_map/all_to_all | solution.py:1047
  1147.4 8.9 copy-start.59
  1147.4 8.9 copy-start.60
  1148.4 12.6 %copy-start.38 = (f32[656,128]{1,0:T(8,128)S(1)}, f32[656,128]{1,0:T(8,128)}, u32[]{:S(2)}) copy-start(f32[656,128]{1,0:T(8,128)} %param.26) | copy-start | bytes 1007620
  1148.4 1.4 collective-permute-start.15
  1149.9 6.4 collective-permute-start.16
  1157.1 1.9 collective-permute-start.17
  1159.0 24.9 %copy-start.2 = (bf16[1,8,4,32,1024]{4,3,0,2,1:T(8,128)(2,1)S(1)}, bf16[1,8,4,32,1024]{4,3,0,2,1:T(8,128)(2,1)}, u32[]{:S(2)}) copy-start(bf16[1,8,4,32,1024]{4,3,0,2,1:T(8,128)(2,1)} %get-tuple-element.325) | copy-start | bytes 6291460
  1159.0 6.1 collective-permute-start.18
  1187.8 9.4 copy-start.34
  1187.8 30.9 %all-to-all-start.11 = ((bf16[8,544,128]{2,1,0:T(8,128)(2,1)}), bf16[8,544,128]{2,1,0:T(8,128)(2,1)S(1)}, u32[]{:S(2)}, u32[]{:S(2)}) async-start(bf16[8,544,128]{2,1,0:T(8,128)(2,1)} %pad_maximum_fusion.4), calls=%async_computation.12 | async-start | bytes 2228224 | tf_op jit(solution)/shard_map/all_to_all | solution.py:921
  1198.3 21.2 %copy-start.25 = (f32[128,768]{0,1:T(8,128)S(1)}, f32[128,768]{0,1:T(8,128)}, u32[]{:S(2)}) copy-start(f32[128,768]{0,1:T(8,128)} %copy-done.24) | copy-start | bytes 1179652
  1199.5 24.5 %copy-start.27 = (f32[128,768]{0,1:T(8,128)S(1)}, f32[128,768]{0,1:T(8,128)}, u32[]{:S(2)}) copy-start(f32[128,768]{0,1:T(8,128)} %copy-done.26) | copy-start | bytes 1179652
  (49 other events, 199.3 us)
Sparse Core Ops, SparseCore 0:
  11.5 72.2 all-gather.5
  87.3 224.5 all-gather.7
  379.3 142.0 all-gather.9
  530.3 248.7 reduce-scatter.1
